TPU v7x, 32 devices: a whole 2x2x4 slice. The times are simulated.
32 devices in a mesh: own: 2 (over x), dom: 16 (over z, y, core).
Axes of the slice: x: 2, y: 2, z: 4, core: 2. Of those that a mesh axis runs over, the one named last changes fastest.
Arguments:
- background: bfloat16 [64, 6, 4096], P(('own', 'dom')), may hold values from -6 to 6
- storm_track: float32 [2, 5], replicated, may hold values from 0.02 to 1638.4, as said below
- need_tiles: int32 [32, 8], P(('own', 'dom')), may hold values from 0 to 63, as said below
- node_cells: int32 [256, 1024], P(('own', 'dom')), may hold values from 0 to 4030, as said below
- node_fracs: float32 [2, 256, 1024], P(None, ('own', 'dom')), may hold values from 0 to 1
- slot_count: int32 [256], P(('own', 'dom')), may hold values from 256 to 1024
- elevation: float32 [2, 131072], P('own', 'dom'), may hold values from 0 to 2
- bed_level: float32 [2, 131072], P('own', 'dom'), may hold values from -1 to 1.5
Outputs:
- forcing: bfloat16 [256, 6, 1024], P(('own', 'dom'))
- surge_level: float32 [2, 131072], P('own', 'dom')
Inputs may be any that keep to these rules, and one draw needn't show every extreme that they name: `need_tiles`: entries k * 4 to (k + 1) * 4 - 1 of a row name tiles of band k (tiles k * 32 to (k + 1) * 32 - 1); within a row the numbers (tile % 32) // 2 are all different. `node_cells`: value // 64 and value % 64 are both at most 62. `storm_track`: row k: centre column and row in cells, pressure deficit, radius of maximum wind in cells, shape exponent; all positive.
All inputs are finite; a program needn't handle non-finite values.
Results may differ from a plain program's by a relative error of at most 0.0023.
The roundings to bfloat16 on the way count: a program that leaves them out, or rounds other values in their place, can miss the bound.
Values may be sent and summed in bfloat16 or wider, within the bound.
A program may use at most 64 MiB of HBM per device.

v0:
```python
import jax
import jax.numpy as jnp
from jax import lax
from jax.sharding import PartitionSpec as P

TILE = 64
TCOLS = 32
TILES_DEV = 2
FIELDS = 6
K_B = 4
SWEEPS = 4


KAPPA = 0.08


def as_sent(value):

    def short(part):
        return part.astype(jnp.bfloat16) if part.dtype == jnp.float32 else part

    return jax.tree.map(short, value)


def extended(cells, sides, width):
    for axis, dim in sides:
        count = lax.axis_size(axis)
        ends = count - 1
        head = lax.slice_in_dim(cells, 0, width, axis=dim)
        tail = lax.slice_in_dim(cells, cells.shape[dim] - width, cells.shape[dim], axis=dim)
        cells = jnp.concatenate(
            [
                lax.ppermute(tail, axis, [(i, (i + 1) % count) for i in range(ends)]),
                cells,
                lax.ppermute(head, axis, [((i + 1) % count, i) for i in range(ends)]),
            ],
            axis=dim,
        )
    return cells


def holland(tile_index, background, storm_track):
    cell_index = jnp.arange(TILE * TILE, dtype=jnp.int32)
    cell_row = (cell_index // TILE).astype(jnp.float32)
    cell_col = (cell_index % TILE).astype(jnp.float32)
    tile_row = (tile_index // TCOLS).astype(jnp.float32)
    tile_col = (tile_index % TCOLS).astype(jnp.float32)
    north_cell = tile_row[:, None] * TILE + cell_row[None, :]
    east_cell = tile_col[:, None] * TILE + cell_col[None, :]
    fields = []
    for time_level in range(2):
        offset_x = east_cell - storm_track[time_level, 0]
        offset_y = north_cell - storm_track[time_level, 1]
        radius = jnp.sqrt(offset_x * offset_x + offset_y * offset_y + 1.0)
        radial_ratio = jnp.exp(
            storm_track[time_level, 4] * jnp.log(storm_track[time_level, 3] / radius)
        )
        pressure_decay = jnp.exp(-radial_ratio)
        wind_speed = jnp.sqrt(
            storm_track[time_level, 4] * storm_track[time_level, 2] * radial_ratio * pressure_decay
        )
        fields.append(-wind_speed * offset_y / radius)
        fields.append(wind_speed * offset_x / radius)
        fields.append(-storm_track[time_level, 2] * (1.0 - pressure_decay))
    return (background.astype(jnp.float32) + jnp.stack(fields, axis=1)).astype(jnp.bfloat16)


def interpolate_local(tile_data, node_cells, node_fracs, slot_count):
    blocks = tile_data.shape[0] // 2
    positions = node_cells.shape[1]
    tile_blocks = tile_data.reshape(blocks, 2, FIELDS * TILE, TILE)
    cell_blocks = node_cells.reshape(blocks, 2, positions)
    frac_blocks = jnp.moveaxis(node_fracs.reshape(2, blocks, 2, positions), 1, 0)
    count_blocks = slot_count.reshape(blocks, 2)
    spot_index = jnp.arange(TILE, dtype=jnp.int32)[None, :, None]
    position_index = jnp.arange(positions, dtype=jnp.int32)

    def one_block(packed):
        tile_block, cell_block, frac_block, count_block = packed
        col_first = (cell_block % TILE)[:, None, :]
        row_first = (cell_block // TILE)[:, None, :]
        east_frac = frac_block[0][:, None, :]
        north_frac = frac_block[1][:, None, :]
        col_weights = (
            jnp.where(spot_index == col_first, 1.0 - east_frac, 0.0)
            + jnp.where(spot_index == col_first + 1, east_frac, 0.0)
        ).astype(jnp.bfloat16)
        row_weights = jnp.where(spot_index == row_first, 1.0 - north_frac, 0.0) + jnp.where(
            spot_index == row_first + 1, north_frac, 0.0
        )
        spread = jnp.einsum(
            "bkj,bjn->bkn", tile_block, col_weights, preferred_element_type=jnp.float32
        )
        node_value = jnp.sum(
            spread.reshape(2, FIELDS, TILE, positions) * row_weights[:, None], axis=2
        )
        live = position_index[None, :] < count_block[:, None]
        return jnp.where(live[:, None, :], node_value, jnp.float32(0.0))

    outputs = lax.map(one_block, (tile_blocks, cell_blocks, frac_blocks, count_blocks))
    return outputs.reshape(blocks * 2, FIELDS, positions)


def flux_sweep_local(elevation, bed_level):
    holders = lax.axis_size("dom")
    position = lax.axis_index("dom")
    length = elevation.shape[1]
    face_index = jnp.arange(length + 1, dtype=jnp.int32)[None, :]
    wall_face = (face_index == 0) & (position == 0) | (face_index == length) & (
        position == holders - 1
    )
    surface = elevation
    for sweep_step in range(SWEEPS):
        padded = extended(as_sent(jnp.stack([surface, bed_level])), (("dom", 2),), 1)
        wet_depth = jnp.maximum(padded[0] - padded[1], 0.0)
        slope_drop = padded[0][:, :-1] - padded[0][:, 1:]
        upwind = jnp.where(slope_drop >= 0.0, wet_depth[:, :-1], wet_depth[:, 1:])
        face_flux = jnp.where(wall_face, jnp.float32(0.0), KAPPA * upwind * slope_drop)
        surface = surface - (face_flux[:, 1:] - face_flux[:, :-1])
    return surface


def shards(
    background, storm_track, need_tiles, node_cells, node_fracs, slot_count, elevation, bed_level
):
    groups = lax.axis_size("own")
    holders = lax.axis_size("dom")
    band_size = TILES_DEV * holders
    device_rank = lax.axis_index("own") * holders + lax.axis_index("dom")
    wanted = need_tiles[0]
    need_count = wanted.shape[0]
    cell_count = TILE * TILE
    own_tiles = device_rank * TILES_DEV + jnp.arange(TILES_DEV, dtype=jnp.int32)
    outgoing = holland(own_tiles, background, storm_track)
    requested = lax.all_to_all(
        wanted.reshape(groups, K_B), "own", split_axis=0, concat_axis=0, tiled=True
    )
    offsets = (requested - lax.axis_index("own") * band_size).reshape(-1)
    empty_rows = jnp.zeros((groups * K_B, FIELDS, cell_count), jnp.bfloat16)
    piece_rows = lax.all_gather(outgoing, "dom", axis=0, tiled=True)
    inside = (offsets >= 0) & (offsets < piece_rows.shape[0])
    chosen = jnp.take(piece_rows, jnp.clip(offsets, 0, piece_rows.shape[0] - 1), axis=0)
    served = jnp.where(inside[:, None, None], chosen, empty_rows)
    arrived = lax.all_to_all(
        served.reshape(groups, K_B, FIELDS, cell_count),
        "own",
        split_axis=0,
        concat_axis=0,
        tiled=True,
    )
    arrived = arrived.reshape(need_count, FIELDS, cell_count)
    values = interpolate_local(arrived, node_cells, node_fracs, slot_count)
    forcing = values.astype(jnp.bfloat16)
    pressure = values[:, 5, :].reshape(1, -1)
    surface = flux_sweep_local(elevation, bed_level)
    surge_level = surface - 0.5 * pressure * jnp.clip(surface - bed_level, 0.0, 1.0)
    return (forcing, surge_level)


def solution(mesh):
    placed = (
        P(("own", "dom"), None, None),
        P(),
        P(("own", "dom"), None),
        P(("own", "dom"), None),
        P(None, ("own", "dom"), None),
        P(("own", "dom")),
        P("own", "dom"),
        P("own", "dom"),
    )
    return jax.shard_map(
        shards,
        mesh=mesh,
        in_specs=placed,
        out_specs=(P(("own", "dom"), None, None), P("own", "dom")),
        check_vma=False,
    )
```

profile of v0, /device:TPU:0, one launch (start us, length us, event | category | flops | bytes accessed | tf_op | source)
XLA Modules:
  0.0 105.6 jit_solution(17441623909516419498)
XLA Ops:
  7.2 1.7 %fusion.73 = (f32[1,1]{1,0:T(1,128)}, f32[1,1]{1,0:T(1,128)}, f32[1,1]{1,0:T(1,128)}, f32[1,1]{1,0:T(1,128)}, f32[1,1]{1,0:T(1,128)}, /*index=5*/f32[1,1]{1,0:T(...) fusion(f32[2,5]{1,0:T(2,128)} %param.11), kind=kLoop, calls=%fused_computation.172 | loop fusion | bytes 80 | tf_op jit(solution)/shard_map/slice | solution.py:60
  10.9 2.8 %divide_dynamic-update-slice_fusion.3 = f32[2,6,4096]{2,0,1:T(2,128)S(1)} fusion(f32[]{:T(128)} %bitcast.6, f32[4096]{0:T(1024)S(1)} %get-tuple-element.232, f32[2]{0:T(128)S(1)} %get-tuple-element.230, f32[]{:T(128)} %bitcast.5, f32[4096]{0:T(1024)S(1)} %get-tuple-element.231, f32[2]{0:T(128)S(1)} %get-tuple-element.229, f32[]{:T(128)} %bitcast.4, ...), kind=kLoop, calls=%fused_computation.108 | loop fusion | flops 131071 | bytes 65572
  13.7 2.8 %divide_dynamic-update-slice_fusion.2 = f32[2,6,4096]{2,0,1:T(2,128)S(1)} fusion(f32[2,6,4096]{2,0,1:T(2,128)S(1)} %divide_dynamic-update-slice_fusion.3, f32[]{:T(128)} %bitcast.5, f32[4096]{0:T(1024)S(1)} %get-tuple-element.231, f32[2]{0:T(128)S(1)} %get-tuple-element.229, f32[]{:T(128)} %bitcast.6, f32[4096]{0:T(1024)S(1)} %get-tuple-element.232, ...), kind=kLoop, calls=%fused_computation.107 | loop fusion | flops 122880 | bytes 66580
  18.4 2.7 %multiply_dynamic-update-slice_fusion.1 = f32[2,6,4096]{2,0,1:T(2,128)S(1)} fusion(f32[2,6,4096]{2,0,1:T(2,128)S(1)} %divide_dynamic-update-slice_fusion.2, f32[]{:T(128)S(6)} %neg.74, f32[]{:T(128)} %bitcast.4, f32[]{:T(128)} %bitcast.2, f32[]{:T(128)} %bitcast.6, f32[4096]{0:T(1024)S(1)} %get-tuple-element.232, f32[2]{0:T(128)S(1)} %get-tuple-element.230, ...), kind=kLoop, calls=%fused_computation.131 | loop fusion | flops 106496 | bytes 66580
  21.2 2.9 %divide_dynamic-update-slice_fusion.1 = f32[2,6,4096]{2,0,1:T(2,128)S(1)} fusion(f32[2,6,4096]{2,0,1:T(2,128)S(1)} %multiply_dynamic-update-slice_fusion.1, f32[]{:T(128)} %bitcast.11, f32[4096]{0:T(1024)S(1)} %get-tuple-element.232, f32[2]{0:T(128)S(1)} %get-tuple-element.230, f32[]{:T(128)} %bitcast.10, f32[4096]{0:T(1024)S(1)} %get-tuple-element.231, ...), kind=kLoop, calls=%fused_computation.106 | loop fusion | flops 131072 | bytes 66580
  24.0 2.9 %divide_dynamic-update-slice_fusion = f32[2,6,4096]{2,0,1:T(2,128)S(1)} fusion(f32[2,6,4096]{2,0,1:T(2,128)S(1)} %divide_dynamic-update-slice_fusion.1, f32[]{:T(128)} %bitcast.10, f32[4096]{0:T(1024)S(1)} %get-tuple-element.231, f32[2]{0:T(128)S(1)} %get-tuple-element.229, f32[]{:T(128)} %bitcast.11, f32[4096]{0:T(1024)S(1)} %get-tuple-element.232, ...), kind=kLoop, calls=%fused_computation.105 | loop fusion | flops 122880 | bytes 66580
  26.9 2.8 %multiply_dynamic-update-slice_fusion = f32[2,6,4096]{2,0,1:T(2,128)S(1)} fusion(f32[2,6,4096]{2,0,1:T(2,128)S(1)} %divide_dynamic-update-slice_fusion, f32[]{:T(128)S(6)} %neg.78, f32[]{:T(128)} %bitcast.9, f32[]{:T(128)} %bitcast.7, f32[]{:T(128)} %bitcast.11, f32[4096]{0:T(1024)S(1)} %get-tuple-element.232, f32[2]{0:T(128)S(1)} %get-tuple-element.230, ...), kind=kLoop, calls=%fused_computation.129 | loop fusion | flops 106496 | bytes 66580 | tf_op jit(solution)/shard_map/stack | solution.py:65
  29.7 1.0 add_convert_fusion.2
  30.7 0.7 copy.33
  31.4 0.5 broadcast.1261
  31.9 1.2 %reduce.6 = s32[8]{0:T(128)S(1)} reduce(s32[1,8]{1,0:T(1,128)} %param.12, s32[]{:T(128)} %broadcast.1261), dimensions={0}, to_apply=%param.12.reduce_sub_computation.3 | reduce | bytes 68 | tf_op args[2]
  33.1 0.6 all_to_all.9
  33.8 4.2 %all-to-all-start = ((s32[2,1,4]{2,1,0:T(1,128)}), s32[2,1,4]{2,1,0:T(1,128)S(1)}, u32[]{:S(2)}, u32[]{:S(2)}) async-start(s32[2,1,4]{2,1,0:T(1,128)} %bitcast), calls=%async_computation | async-start | bytes 2048 | tf_op jit(solution)/shard_map/all_to_all | solution.py:135
  38.0 0.8 convert_bitcast_fusion
  38.9 1.4 %collective-permute-start = (bf16[2,1,1]{2,1,0:T(2,128)(2,1)S(1)}, bf16[2,1,1]{2,1,0:T(2,128)(2,1)S(1)}, u32[]{:S(2)}, u32[]{:S(2)}) collective-permute-start(bf16[2,1,1]{2,1,0:T(2,128)(2,1)S(1)} %get-tuple-element.218), channel_id=1, source_target_pairs={{0,1},{1,2},{2,3},{3,4},{4,5},{5,6},{6,7},{7,8},{8,9},{9,10},{10,1... | collective-permute-start | bytes 20 | tf_op jit(solution)/shard_map/ppermute | solution.py:33
  40.4 1.3 %collective-permute-start.1 = (bf16[2,1,1]{2,1,0:T(2,128)(2,1)S(1)}, bf16[2,1,1]{2,1,0:T(2,128)(2,1)S(1)}, u32[]{:S(2)}, u32[]{:S(2)}) collective-permute-start(bf16[2,1,1]{2,1,0:T(2,128)(2,1)S(1)} %get-tuple-element.217), channel_id=1, source_target_pairs={{1,0},{2,1},{3,2},{4,3},{5,4},{6,5},{7,6},{8,7},{9,8},{10,9},{11,1... | collective-permute-start | bytes 20 | tf_op jit(solution)/shard_map/ppermute | solution.py:35
  41.8 0.7 reshape.1199
  42.5 0.8 reshape.1200
  43.3 0.9 copy.36
  44.2 1.2 %collective-permute-done.1 = bf16[2,1,1]{2,1,0:T(2,128)(2,1)S(1)} collective-permute-done((bf16[2,1,1]{2,1,0:T(2,128)(2,1)S(1)}, bf16[2,1,1]{2,1,0:T(2,128)(2,1)S(1)}, u32[]{:S(2)}, u32[]{:S(2)}) %collective-permute-start.1) | collective-permute-done | bytes 36 | tf_op jit(solution)/shard_map/ppermute | solution.py:35
  46.0 0.9 convert_bitcast_fusion.3
  47.1 4.3 %collective-permute-start.2 = (bf16[2,1,1]{2,1,0:T(2,128)(2,1)S(1)}, bf16[2,1,1]{2,1,0:T(2,128)(2,1)S(1)}, u32[]{:S(2)}, u32[]{:S(2)}) collective-permute-start(bf16[2,1,1]{2,1,0:T(2,128)(2,1)S(1)} %get-tuple-element.216), channel_id=1, source_target_pairs={{0,1},{1,2},{2,3},{3,4},{4,5},{5,6},{6,7},{7,8},{8,9},{9,10},{10,1... | collective-permute-start | bytes 20 | tf_op jit(solution)/shard_map/ppermute | solution.py:33
  51.4 1.3 %collective-permute-start.3 = (bf16[2,1,1]{2,1,0:T(2,128)(2,1)S(1)}, bf16[2,1,1]{2,1,0:T(2,128)(2,1)S(1)}, u32[]{:S(2)}, u32[]{:S(2)}) collective-permute-start(bf16[2,1,1]{2,1,0:T(2,128)(2,1)S(1)} %get-tuple-element.215), channel_id=1, source_target_pairs={{1,0},{2,1},{3,2},{4,3},{5,4},{6,5},{7,6},{8,7},{9,8},{10,9},{11,1... | collective-permute-start | bytes 20 | tf_op jit(solution)/shard_map/ppermute | solution.py:35
  52.7 2.6 %collective-permute-done.3 = bf16[2,1,1]{2,1,0:T(2,128)(2,1)S(1)} collective-permute-done((bf16[2,1,1]{2,1,0:T(2,128)(2,1)S(1)}, bf16[2,1,1]{2,1,0:T(2,128)(2,1)S(1)}, u32[]{:S(2)}, u32[]{:S(2)}) %collective-permute-start.3) | collective-permute-done | bytes 36 | tf_op jit(solution)/shard_map/ppermute | solution.py:35
  56.2 4.3 %collective-permute-start.4 = (bf16[2,1,1]{2,1,0:T(2,128)(2,1)S(1)}, bf16[2,1,1]{2,1,0:T(2,128)(2,1)S(1)}, u32[]{:S(2)}, u32[]{:S(2)}) collective-permute-start(bf16[2,1,1]{2,1,0:T(2,128)(2,1)S(1)} %get-tuple-element.214), channel_id=1, source_target_pairs={{0,1},{1,2},{2,3},{3,4},{4,5},{5,6},{6,7},{7,8},{8,9},{9,10},{10,1... | collective-permute-start | bytes 20 | tf_op jit(solution)/shard_map/ppermute | solution.py:33
  60.5 1.3 %collective-permute-start.5 = (bf16[2,1,1]{2,1,0:T(2,128)(2,1)S(1)}, bf16[2,1,1]{2,1,0:T(2,128)(2,1)S(1)}, u32[]{:S(2)}, u32[]{:S(2)}) collective-permute-start(bf16[2,1,1]{2,1,0:T(2,128)(2,1)S(1)} %get-tuple-element.213), channel_id=1, source_target_pairs={{1,0},{2,1},{3,2},{4,3},{5,4},{6,5},{7,6},{8,7},{9,8},{10,9},{11,1... | collective-permute-start | bytes 20 | tf_op jit(solution)/shard_map/ppermute | solution.py:35
  61.8 1.7 %collective-permute-done.5 = bf16[2,1,1]{2,1,0:T(2,128)(2,1)S(1)} collective-permute-done((bf16[2,1,1]{2,1,0:T(2,128)(2,1)S(1)}, bf16[2,1,1]{2,1,0:T(2,128)(2,1)S(1)}, u32[]{:S(2)}, u32[]{:S(2)}) %collective-permute-start.5) | collective-permute-done | bytes 36 | tf_op jit(solution)/shard_map/ppermute | solution.py:35
  64.5 5.9 %collective-permute-start.6 = (bf16[2,1,1]{2,1,0:T(2,128)(2,1)S(1)}, bf16[2,1,1]{2,1,0:T(2,128)(2,1)S(1)}, u32[]{:S(2)}, u32[]{:S(2)}) collective-permute-start(bf16[2,1,1]{2,1,0:T(2,128)(2,1)S(1)} %get-tuple-element.212), channel_id=1, source_target_pairs={{0,1},{1,2},{2,3},{3,4},{4,5},{5,6},{6,7},{7,8},{8,9},{9,10},{10,1... | collective-permute-start | bytes 20 | tf_op jit(solution)/shard_map/ppermute | solution.py:33
  70.4 1.3 %collective-permute-start.7 = (bf16[2,1,1]{2,1,0:T(2,128)(2,1)S(1)}, bf16[2,1,1]{2,1,0:T(2,128)(2,1)S(1)}, u32[]{:S(2)}, u32[]{:S(2)}) collective-permute-start(bf16[2,1,1]{2,1,0:T(2,128)(2,1)S(1)} %get-tuple-element.211), channel_id=1, source_target_pairs={{1,0},{2,1},{3,2},{4,3},{5,4},{6,5},{7,6},{8,7},{9,8},{10,9},{11,1... | collective-permute-start | bytes 20 | tf_op jit(solution)/shard_map/ppermute | solution.py:35
  71.7 1.7 %collective-permute-done.7 = bf16[2,1,1]{2,1,0:T(2,128)(2,1)S(1)} collective-permute-done((bf16[2,1,1]{2,1,0:T(2,128)(2,1)S(1)}, bf16[2,1,1]{2,1,0:T(2,128)(2,1)S(1)}, u32[]{:S(2)}, u32[]{:S(2)}) %collective-permute-start.7) | collective-permute-done | bytes 36 | tf_op jit(solution)/shard_map/ppermute | solution.py:35
  73.8 0.6 fusion.72
  74.6 1.1 %all-gather.2.cloned.1.call-done = bf16[32,6,4096]{2,1,0:T(8,128)(2,1)} async-done(((bf16[2,6,4096]{2,1,0:T(8,128)(2,1)}), bf16[32,6,4096]{2,1,0:T(8,128)(2,1)}) %all-gather.2.cloned.1.call-update) | async-done | bytes 1572880 | tf_op jit(solution)/shard_map/all_gather | solution.py:140
  75.7 2.2 %gather_fusion = bf16[8,6,4096]{2,1,0:T(8,128)(2,1)S(1)} fusion(bf16[32,6,4096]{2,1,0:T(8,128)(2,1)} %all-gather.2.cloned.1.call-done, s32[1024]{0:T(1024)S(1)} %pad_clamp_fusion), kind=kCustom, calls=%fused_computation | custom fusion | bytes 786464 | tf_op jit(solution)/shard_map/jit(_take)/gather | solution.py:142
  77.8 1.1 %fusion.16 = bf16[2,4,6,4096]{3,1,2,0:T(4,128)(2,1)} fusion(bf16[2,4,6,4096]{3,2,1,0:T(8,128)(2,1)S(1)} %bitcast.129, pred[2,4]{1,0:T(4,128)(4,1)S(1)} %compare_and_fusion.1, pred[2,4]{1,0:T(4,128)(4,1)S(1)} %bitcast.134), kind=kLoop, calls=%fused_computation.42 | loop fusion | flops 393216 | bytes 786448 | tf_op jit(solution)/shard_map/jit(_where)/select_n | solution.py:143
  79.0 3.5 %all-to-all-start.1 = ((bf16[2,4,6,4096]{3,1,2,0:T(4,128)(2,1)}), bf16[2,4,6,4096]{3,1,2,0:T(4,128)(2,1)S(1)}, u32[]{:S(2)}, u32[]{:S(2)}) async-start(bf16[2,4,6,4096]{3,1,2,0:T(4,128)(2,1)} %fusion.16), calls=%async_computation.1 | async-start | bytes 786432 | tf_op jit(solution)/shard_map/all_to_all | solution.py:144
  82.6 7.1 %all-to-all-done.1 = bf16[2,4,6,4096]{3,1,2,0:T(4,128)(2,1)S(1)} async-done(((bf16[2,4,6,4096]{3,1,2,0:T(4,128)(2,1)}), bf16[2,4,6,4096]{3,1,2,0:T(4,128)(2,1)S(1)}, u32[]{:S(2)}, u32[]{:S(2)}) %all-to-all-start.1) | async-done | bytes 393248 | tf_op jit(solution)/shard_map/all_to_all | solution.py:144
  90.0 0.9 reshape_reshape.3
  91.2 5.9 %while.14 = (s32[]{:T(128)}, f32[4,2,6,1024]{3,2,1,0:T(8,128)S(1)}, s32[4,2]{1,0:T(4,128)S(1)}, bf16[4,2,384,64]{2,3,1,0:T(8,128)(2,1)S(1)}, s32[4,2,1024]{2,1,0...) while((s32[]{:T(128)}, f32[4,2,6,1024]{3,2,1,0:T(8,128)S(1)}, ...), condition=%wide.region_2.3_spmd.clone.clone, body=%wide.region_0.2_spmd.clone.clone.sunk | while | flops 103727104 | bytes 7829665 | solution.py:100
  91.3 0.6 fusion.79
  92.1 0.5 multiply_reduce_fusion.2
  92.8 0.6 fusion.79
  93.5 0.5 multiply_reduce_fusion.2
  94.3 0.6 fusion.79
  95.0 0.5 multiply_reduce_fusion.2
  95.8 0.6 fusion.79
  96.5 0.5 multiply_reduce_fusion.2
  97.1 0.8 fusion.71
  98.0 0.8 multiply_subtract_fusion
  (80 shorter events, 5.3 us)
Async XLA Ops:
  7.2 68.5 %all-gather.2.cloned.1.call-start = ((), (), s32[]{:S(2)}) async-start(), calls=%async_computation.2 | async-start | bytes 2228224 | tf_op jit(solution)/shard_map/all_gather | solution.py:140
  33.8 40.0 %all-to-all-start = ((s32[2,1,4]{2,1,0:T(1,128)}), s32[2,1,4]{2,1,0:T(1,128)S(1)}, u32[]{:S(2)}, u32[]{:S(2)}) async-start(s32[2,1,4]{2,1,0:T(1,128)} %bitcast), calls=%async_computation | async-start | bytes 2048 | tf_op jit(solution)/shard_map/all_to_all | solution.py:135
  38.9 5.3 %collective-permute-start = (bf16[2,1,1]{2,1,0:T(2,128)(2,1)S(1)}, bf16[2,1,1]{2,1,0:T(2,128)(2,1)S(1)}, u32[]{:S(2)}, u32[]{:S(2)}) collective-permute-start(bf16[2,1,1]{2,1,0:T(2,128)(2,1)S(1)} %get-tuple-element.218), channel_id=1, source_target_pairs={{0,1},{1,2},{2,3},{3,4},{4,5},{5,6},{6,7},{7,8},{8,9},{9,10},{10,1... | collective-permute-start | bytes 20 | tf_op jit(solution)/shard_map/ppermute | solution.py:33
  40.4 5.1 %collective-permute-start.1 = (bf16[2,1,1]{2,1,0:T(2,128)(2,1)S(1)}, bf16[2,1,1]{2,1,0:T(2,128)(2,1)S(1)}, u32[]{:S(2)}, u32[]{:S(2)}) collective-permute-start(bf16[2,1,1]{2,1,0:T(2,128)(2,1)S(1)} %get-tuple-element.217), channel_id=1, source_target_pairs={{1,0},{2,1},{3,2},{4,3},{5,4},{6,5},{7,6},{8,7},{9,8},{10,9},{11,1... | collective-permute-start | bytes 20 | tf_op jit(solution)/shard_map/ppermute | solution.py:35
  47.1 5.6 %collective-permute-start.2 = (bf16[2,1,1]{2,1,0:T(2,128)(2,1)S(1)}, bf16[2,1,1]{2,1,0:T(2,128)(2,1)S(1)}, u32[]{:S(2)}, u32[]{:S(2)}) collective-permute-start(bf16[2,1,1]{2,1,0:T(2,128)(2,1)S(1)} %get-tuple-element.216), channel_id=1, source_target_pairs={{0,1},{1,2},{2,3},{3,4},{4,5},{5,6},{6,7},{7,8},{8,9},{9,10},{10,1... | collective-permute-start | bytes 20 | tf_op jit(solution)/shard_map/ppermute | solution.py:33
  51.4 3.9 %collective-permute-start.3 = (bf16[2,1,1]{2,1,0:T(2,128)(2,1)S(1)}, bf16[2,1,1]{2,1,0:T(2,128)(2,1)S(1)}, u32[]{:S(2)}, u32[]{:S(2)}) collective-permute-start(bf16[2,1,1]{2,1,0:T(2,128)(2,1)S(1)} %get-tuple-element.215), channel_id=1, source_target_pairs={{1,0},{2,1},{3,2},{4,3},{5,4},{6,5},{7,6},{8,7},{9,8},{10,9},{11,1... | collective-permute-start | bytes 20 | tf_op jit(solution)/shard_map/ppermute | solution.py:35
  56.2 5.6 %collective-permute-start.4 = (bf16[2,1,1]{2,1,0:T(2,128)(2,1)S(1)}, bf16[2,1,1]{2,1,0:T(2,128)(2,1)S(1)}, u32[]{:S(2)}, u32[]{:S(2)}) collective-permute-start(bf16[2,1,1]{2,1,0:T(2,128)(2,1)S(1)} %get-tuple-element.214), channel_id=1, source_target_pairs={{0,1},{1,2},{2,3},{3,4},{4,5},{5,6},{6,7},{7,8},{8,9},{9,10},{10,1... | collective-permute-start | bytes 20 | tf_op jit(solution)/shard_map/ppermute | solution.py:33
  60.5 3.0 %collective-permute-start.5 = (bf16[2,1,1]{2,1,0:T(2,128)(2,1)S(1)}, bf16[2,1,1]{2,1,0:T(2,128)(2,1)S(1)}, u32[]{:S(2)}, u32[]{:S(2)}) collective-permute-start(bf16[2,1,1]{2,1,0:T(2,128)(2,1)S(1)} %get-tuple-element.213), channel_id=1, source_target_pairs={{1,0},{2,1},{3,2},{4,3},{5,4},{6,5},{7,6},{8,7},{9,8},{10,9},{11,1... | collective-permute-start | bytes 20 | tf_op jit(solution)/shard_map/ppermute | solution.py:35
  64.5 7.2 %collective-permute-start.6 = (bf16[2,1,1]{2,1,0:T(2,128)(2,1)S(1)}, bf16[2,1,1]{2,1,0:T(2,128)(2,1)S(1)}, u32[]{:S(2)}, u32[]{:S(2)}) collective-permute-start(bf16[2,1,1]{2,1,0:T(2,128)(2,1)S(1)} %get-tuple-element.212), channel_id=1, source_target_pairs={{0,1},{1,2},{2,3},{3,4},{4,5},{5,6},{6,7},{7,8},{8,9},{9,10},{10,1... | collective-permute-start | bytes 20 | tf_op jit(solution)/shard_map/ppermute | solution.py:33
  70.4 3.0 %collective-permute-start.7 = (bf16[2,1,1]{2,1,0:T(2,128)(2,1)S(1)}, bf16[2,1,1]{2,1,0:T(2,128)(2,1)S(1)}, u32[]{:S(2)}, u32[]{:S(2)}) collective-permute-start(bf16[2,1,1]{2,1,0:T(2,128)(2,1)S(1)} %get-tuple-element.211), channel_id=1, source_target_pairs={{1,0},{2,1},{3,2},{4,3},{5,4},{6,5},{7,6},{8,7},{9,8},{10,9},{11,1... | collective-permute-start | bytes 20 | tf_op jit(solution)/shard_map/ppermute | solution.py:35
  79.0 10.8 %all-to-all-start.1 = ((bf16[2,4,6,4096]{3,1,2,0:T(4,128)(2,1)}), bf16[2,4,6,4096]{3,1,2,0:T(4,128)(2,1)S(1)}, u32[]{:S(2)}, u32[]{:S(2)}) async-start(bf16[2,4,6,4096]{3,1,2,0:T(4,128)(2,1)} %fusion.16), calls=%async_computation.1 | async-start | bytes 786432 | tf_op jit(solution)/shard_map/all_to_all | solution.py:144
  91.2 6.8 %copy-start = (f32[1,8192]{1,0:T(1,128)S(1)}, f32[1,8192]{1,0:T(1,128)}, u32[]{:S(2)}) copy-start(f32[1,8192]{1,0:T(1,128)} %param.17) | copy-start | bytes 98308
Sparse Core Ops, SparseCore 0:
  31.5 44.0 all-gather.1
where the time goes:
time: 107 us; the launch traced here: 106 us
  other arithmetic  29 us (27%)
  starting transfers between devices  28.7 us (27%)
  between operations  18.3 us (17%)
  waiting for transfers between devices  15.5 us (14%)
  local copies, waits for them, and re-layouts  11.2 us (10%)
  matrix products  2.49 us (2%)
    ppermute x4, starting transfers between devices, extended(): lax.ppermute(tail, axis, [(i, (i + 1) % count) for i in range(ends)])  15.8 us
    unnamed x7, other arithmetic  15.2 us
    ppermute x4, waiting for transfers between devices, extended(): lax.ppermute(head, axis, [((i + 1) % count, i) for i in range(ends)])  7.23 us
    all_to_all x1, waiting for transfers between devices, shards(): lax.all_to_all(served.reshape(groups, K_B, FIELDS, cell_count), 'own', sp...  7.14 us
    ppermute x4, starting transfers between devices, extended(): lax.ppermute(head, axis, [((i + 1) % count, i) for i in range(ends)])  5.17 us
    all_to_all x1, starting transfers between devices, shards(): lax.all_to_all(wanted.reshape(groups, K_B), 'own', split_axis=0, concat_a...  4.21 us
    all_to_all x1, starting transfers between devices, shards(): lax.all_to_all(served.reshape(groups, K_B, FIELDS, cell_count), 'own', sp...  3.46 us
    another operation x1, other arithmetic, holland(): jnp.stack(fields, axis=1)  2.77 us
  transfers between devices with their start and end apart: 11, of which 6 were waited for; matrix products, arithmetic and copies ran while one was open for 9% of the time, Pallas kernels for 0%

commit v1 on v0

v1 whole, which is shorter than its diff:
```python
import functools

import jax
import jax.numpy as jnp
from jax import lax
from jax.experimental import pallas as pl
from jax.experimental.pallas import tpu as pltpu
from jax.sharding import PartitionSpec as P

TILE = 64
TCOLS = 32
SWEEPS = 4
KAPPA = 0.08
LANES = 128
HALO = 8


def kernel(
    groups, holders,
    storm_ref, need_ref, count_ref, back_ref, cells_ref, fracs_ref, elev_ref, bed_ref,
    forcing_ref, surge_ref,
    grid_ref, field_ref, data_ref, node_out_ref, need_out_ref, need_in_ref, need_smem,
    colw_ref, roww_ref, surf_ref, ground_ref, press_ref, res_out_ref, res_in_ref,
    ring_send, ring_recv, sib_send, sib_recv, halo_send, halo_recv,
    node_send, node_recv, need_send, need_recv, need_local, res_send, res_recv,
):
    own = lax.axis_index("own")
    dom = lax.axis_index("dom")
    tiles_dev, fields, cell_count = back_ref.shape
    slots, positions = cells_ref.shape
    per_band = slots // groups
    pairs = cell_count // LANES
    chips = holders // 2
    half = chips // 2
    band = tiles_dev * holders

    core = dom % 2
    chip = dom // 2
    odd = chip % 2
    place = (chip // 2) * (1 - odd) + (chips - 1 - chip // 2) * odd

    def device_at(where, which_core):
        where = (where + chips) % chips
        back = where // half
        at_chip = (2 * where) * (1 - back) + (2 * (chips - 1 - where) + 1) * back
        return at_chip * 2 + which_core

    right = device_at(place + 1, core)
    left = device_at(place - 1, core)
    sibling = chip * 2 + 1 - core
    after = (dom + 1) % holders
    before = (dom + holders - 1) % holders

    barrier = pltpu.get_barrier_semaphore()
    for neighbour in (right, left, sibling, after, before):
        pl.semaphore_signal(barrier, inc=1, device_id={"dom": neighbour})
    for j in range(1, groups):
        pl.semaphore_signal(barrier, inc=1, device_id={"own": (own + j) % groups})

    pair_index = lax.broadcasted_iota(jnp.int32, (pairs, LANES), 0)
    lane_index = lax.broadcasted_iota(jnp.int32, (pairs, LANES), 1)
    cell_row = (pair_index * (LANES // TILE) + lane_index // TILE).astype(jnp.float32)
    cell_col = (lane_index % TILE).astype(jnp.float32)
    for t in range(tiles_dev):
        for p in range(pairs):
            field_ref[pl.ds(p, fields, stride=pairs), :] = back_ref[
                t, :, p * LANES : (p + 1) * LANES
            ].astype(jnp.float32)
        tile = own * band + dom * tiles_dev + t
        north = (tile // TCOLS * TILE).astype(jnp.float32) + cell_row
        east = (tile % TCOLS * TILE).astype(jnp.float32) + cell_col
        mine = grid_ref.at[dom * tiles_dev + t]
        for k in range(2):
            offset_x = east - storm_ref[k, 0]
            offset_y = north - storm_ref[k, 1]
            deficit = storm_ref[k, 2]
            shape = storm_ref[k, 4]
            radius = jnp.sqrt(offset_x * offset_x + offset_y * offset_y + 1.0)
            ratio = jnp.exp(shape * jnp.log(storm_ref[k, 3] / radius))
            decay = jnp.exp(-ratio)
            speed = jnp.sqrt(shape * deficit * ratio * decay)
            added = (
                -speed * offset_y / radius,
                speed * offset_x / radius,
                -deficit * (1.0 - decay),
            )
            for m, term in enumerate(added):
                rows = pl.ds((3 * k + m) * pairs, pairs)
                mine[rows, :] = (field_ref[rows, :] + term).astype(jnp.bfloat16)

    pl.semaphore_wait(barrier, 5 + groups - 1)

    def tile_of(where, which_core, t):
        return grid_ref.at[device_at(where, which_core) * tiles_dev + t]

    def ring_copy(way, far, t):
        where = place - far + 1 if way == 0 else place + far - 1
        ref = tile_of(where, core, t)
        return pltpu.make_async_remote_copy(
            src_ref=ref, dst_ref=ref,
            send_sem=ring_send.at[way, far - 1, t], recv_sem=ring_recv.at[way, far - 1, t],
            device_id={"dom": right if way == 0 else left},
        )

    def ring_arrival(way, far, t):
        where = place - far if way == 0 else place + far
        ref = tile_of(where, core, t)
        return pltpu.make_async_remote_copy(
            src_ref=ref, dst_ref=ref,
            send_sem=ring_send.at[way, far - 1, t], recv_sem=ring_recv.at[way, far - 1, t],
            device_id={"dom": right if way == 0 else left},
        )

    def sibling_copy(way, far, t, which_core):
        where = place - far if way == 0 else place + far
        ref = tile_of(where, which_core, t)
        return pltpu.make_async_remote_copy(
            src_ref=ref, dst_ref=ref,
            send_sem=sib_send.at[way, far, t], recv_sem=sib_recv.at[way, far, t],
            device_id={"dom": sibling},
        )

    def reach(way, t):
        return half if t % 2 == way else half - 1

    sent = []

    def start(copy):
        copy.start()
        sent.append(copy)

    first = [(way, (way + s) % tiles_dev) for s in range(tiles_dev) for way in range(2)]
    for way, t in first:
        if reach(way, t) >= 1:
            start(ring_copy(way, 1, t))
    for t in range(tiles_dev):
        start(sibling_copy(0, 0, t, core))

    length = elev_ref.shape[0]
    ends = ((after, length - HALO, 0, 0), (before, 0, HALO + length, 1))
    halo = []
    for target, source_row, target_row, side in ends:
        for m, (source, target_ref) in enumerate(((elev_ref, surf_ref), (bed_ref, ground_ref))):
            copy = pltpu.make_async_remote_copy(
                src_ref=source.at[pl.ds(source_row, HALO)],
                dst_ref=target_ref.at[pl.ds(target_row, HALO)],
                send_sem=halo_send.at[side, m], recv_sem=halo_recv.at[side, m],
                device_id={"dom": target},
            )
            start(copy)
            halo.append(copy)

    live_index = lax.broadcasted_iota(jnp.int32, (1, positions), 1)
    row_index = lax.broadcasted_iota(jnp.int32, (8, LANES), 0)

    def node_rows(j, target):
        group = (own + j) % groups
        for i in range(per_band):
            slot = group * per_band + i
            live = live_index < count_ref[slot]
            north_frac = fracs_ref[1, pl.ds(slot, 1), :]
            target[pl.ds(i, 1), :] = cells_ref[pl.ds(slot, 1), :].astype(jnp.float32)
            target[pl.ds(per_band + i, 1), :] = fracs_ref[0, pl.ds(slot, 1), :]
            target[pl.ds(2 * per_band + i, 1), :] = jnp.where(live, 1.0 - north_frac, 0.0)
            target[pl.ds(3 * per_band + i, 1), :] = jnp.where(live, north_frac, 0.0)

    asked = []
    for j in range(1, groups):
        group = (own + j) % groups
        node_rows(j, node_out_ref.at[j - 1])
        wanted = jnp.zeros((8, LANES), jnp.int32)
        for i in range(per_band):
            wanted = jnp.where(row_index == i, need_ref[0, group * per_band + i], wanted)
        need_out_ref[j - 1] = wanted
        node = pltpu.make_async_remote_copy(
            src_ref=node_out_ref.at[j - 1], dst_ref=data_ref.at[j],
            send_sem=node_send.at[j], recv_sem=node_recv.at[j],
            device_id={"own": group},
        )
        start(node)
        need = pltpu.make_async_remote_copy(
            src_ref=need_out_ref.at[j - 1], dst_ref=need_in_ref.at[j - 1],
            send_sem=need_send.at[j], recv_sem=need_recv.at[j],
            device_id={"own": group},
        )
        start(need)
        asked.append((node, need))
    node_rows(0, data_ref.at[0])

    col_index = lax.broadcasted_iota(jnp.int32, (TILE, positions), 0)
    even_index = lax.broadcasted_iota(jnp.int32, (pairs, positions), 0) * 2

    def weights(j, i):
        cells = data_ref[j, pl.ds(i, 1), :].astype(jnp.int32)
        east_frac = data_ref[j, pl.ds(per_band + i, 1), :]
        upper = data_ref[j, pl.ds(2 * per_band + i, 1), :]
        lower = data_ref[j, pl.ds(3 * per_band + i, 1), :]
        col_first = cells % TILE
        row_first = cells // TILE
        colw_ref[j * per_band + i] = jnp.where(
            col_index == col_first, 1.0 - east_frac,
            jnp.where(col_index == col_first + 1, east_frac, 0.0),
        ).astype(jnp.bfloat16)
        for h in range(2):
            row = even_index + h
            roww_ref[j * per_band + i, h] = jnp.where(
                row == row_first, upper, jnp.where(row == row_first + 1, lower, 0.0)
            )

    def await_asked(j):
        node, need = asked[j - 1]
        need.wait_recv()
        local = pltpu.make_async_copy(
            need_in_ref.at[j - 1], need_smem.at[j - 1], need_local.at[j]
        )
        local.start()
        node.wait_recv()
        local.wait()

    def sweep():
        surf_ref[pl.ds(HALO, length), :] = elev_ref[...]
        ground_ref[pl.ds(HALO, length), :] = bed_ref[...]
        for copy in halo:
            copy.wait_recv()
        surface = surf_ref[...]
        ground = ground_ref[...]
        rows = length + 2 * HALO
        row = lax.broadcasted_iota(jnp.int32, (rows, LANES), 0)
        lane = lax.broadcasted_iota(jnp.int32, (rows, LANES), 1)
        wall = ((row == HALO - 1) & (lane == LANES - 1) & (dom == 0)) | (
            (row == HALO + length - 1) & (lane == LANES - 1) & (dom == holders - 1)
        )

        def shifted(values, by):
            turned = pltpu.roll(values, by % LANES, 1)
            other = pltpu.roll(turned, by % rows, 0)
            edge = lane == (0 if by == 1 else LANES - 1)
            return jnp.where(edge, other, turned)

        for _ in range(SWEEPS):
            wet = jnp.maximum(surface - ground, 0.0)
            drop = surface - shifted(surface, -1)
            upwind = jnp.where(drop >= 0.0, wet, shifted(wet, -1))
            flux = jnp.where(wall, 0.0, KAPPA * upwind * drop)
            surface = surface - (flux - shifted(flux, 1))
        surf_ref[...] = surface

    work = [functools.partial(weights, 0, i) for i in range(per_band)]
    for j in range(1, groups):
        work.append(functools.partial(await_asked, j))
        work += [functools.partial(weights, j, i) for i in range(per_band)]
    work.append(sweep)

    events = [
        (way, far, t)
        for far in range(1, half + 1)
        for way, t in first
        if far <= reach(way, t)
    ]
    done = 0
    for n, (way, far, t) in enumerate(events):
        until = (n + 1) * len(work) // len(events)
        for item in work[done:until]:
            item()
        done = until
        ring_arrival(way, far, t).wait_recv()
        if far < reach(way, t):
            start(ring_copy(way, far + 1, t))
        start(sibling_copy(way, far, t, core))
    for t in range(tiles_dev):
        sibling_copy(0, 0, t, 1 - core).wait_recv()
    for way, far, t in events:
        sibling_copy(way, far, t, 1 - core).wait_recv()

    chunk = 256

    def node_values(j, i, tile):
        cells = grid_ref[lax.rem(tile, band)]
        slot = j * per_band + i
        parts = []
        for n in range(positions // chunk):
            cut = pl.ds(n * chunk, chunk)
            total = None
            for h in range(2):
                spread = jnp.dot(
                    cells[:, h * TILE : (h + 1) * TILE], colw_ref[slot, :, cut],
                    preferred_element_type=jnp.float32,
                )
                part = spread.reshape(fields, pairs, chunk) * roww_ref[slot, h, :, cut][None]
                total = part if total is None else total + part
            parts.append(jnp.sum(total, axis=1))
        return jnp.concatenate(parts, axis=1)

    def keep_pressure(slot, pressure):
        for m in range(positions // LANES):
            press_ref[pl.ds(slot * (positions // LANES) + m, 1), :] = pressure[
                :, m * LANES : (m + 1) * LANES
            ]

    answers = []
    for j in range(1, groups):
        for m in range(per_band // 2):
            rows = []
            for i in (2 * m, 2 * m + 1):
                value = node_values(j, i, need_smem[j - 1, i, 0])
                pressure = value[fields - 1 : fields]
                rest = pressure - pressure.astype(jnp.bfloat16).astype(jnp.float32)
                rows += [value, rest, jnp.zeros((8 - fields - 1, positions), jnp.float32)]
            res_out_ref[j - 1, m] = jnp.concatenate(rows, axis=0).astype(jnp.bfloat16)
            copy = pltpu.make_async_remote_copy(
                src_ref=res_out_ref.at[j - 1, m], dst_ref=res_in_ref.at[j - 1, m],
                send_sem=res_send.at[j - 1, m], recv_sem=res_recv.at[j - 1, m],
                device_id={"own": (own + groups - j) % groups},
            )
            start(copy)
            answers.append((j, m, copy))
    for i in range(per_band):
        slot = own * per_band + i
        value = node_values(0, i, need_ref[0, slot])
        forcing_ref[slot] = value.astype(jnp.bfloat16)
        keep_pressure(slot, value[fields - 1 : fields])
    for j, m, copy in answers:
        copy.wait_recv()
        got = res_in_ref[j - 1, m].astype(jnp.float32)
        for i in range(2):
            slot = (own + j) % groups * per_band + 2 * m + i
            value = got[8 * i : 8 * i + fields]
            forcing_ref[slot] = value.astype(jnp.bfloat16)
            keep_pressure(
                slot, got[8 * i + fields - 1 : 8 * i + fields] + got[8 * i + fields : 8 * i + fields + 1]
            )
    surface = surf_ref[pl.ds(HALO, length), :]
    surge_ref[...] = surface - 0.5 * press_ref[...] * jnp.clip(surface - bed_ref[...], 0.0, 1.0)
    for copy in sent:
        copy.wait_send()


def shards(
    background, storm_track, need_tiles, node_cells, node_fracs, slot_count, elevation, bed_level
):
    groups = lax.axis_size("own")
    holders = lax.axis_size("dom")
    tiles_dev, fields, cell_count = background.shape
    slots, positions = node_cells.shape
    per_band = slots // groups
    chips = holders // 2
    half = chips // 2
    pairs = cell_count // LANES
    length = elevation.shape[1] // LANES
    others = max(groups - 1, 1)
    vmem = pl.BlockSpec(memory_space=pltpu.VMEM)
    smem = pl.BlockSpec(memory_space=pltpu.SMEM)
    dma = pltpu.SemaphoreType.DMA
    forcing, surge = pl.pallas_call(
        functools.partial(kernel, groups, holders),
        out_shape=(
            jax.ShapeDtypeStruct((slots, fields, positions), jnp.bfloat16),
            jax.ShapeDtypeStruct((length, LANES), jnp.float32),
        ),
        in_specs=[smem] * 3 + [vmem] * 5,
        out_specs=(vmem, vmem),
        scratch_shapes=[
            pltpu.VMEM((tiles_dev * holders, fields * pairs, LANES), jnp.bfloat16),
            pltpu.VMEM((fields * pairs, LANES), jnp.float32),
            pltpu.VMEM((groups, 4 * per_band, positions), jnp.float32),
            pltpu.VMEM((others, 4 * per_band, positions), jnp.float32),
            pltpu.VMEM((others, 8, LANES), jnp.int32),
            pltpu.VMEM((others, 8, LANES), jnp.int32),
            pltpu.SMEM((others, 8, LANES), jnp.int32),
            pltpu.VMEM((slots, TILE, positions), jnp.bfloat16),
            pltpu.VMEM((slots, 2, pairs, positions), jnp.float32),
            pltpu.VMEM((length + 2 * HALO, LANES), jnp.float32),
            pltpu.VMEM((length + 2 * HALO, LANES), jnp.float32),
            pltpu.VMEM((length, LANES), jnp.float32),
            pltpu.VMEM((others, per_band // 2, 16, positions), jnp.bfloat16),
            pltpu.VMEM((others, per_band // 2, 16, positions), jnp.bfloat16),
            dma((2, half, tiles_dev)), dma((2, half, tiles_dev)),
            dma((2, half + 1, tiles_dev)), dma((2, half + 1, tiles_dev)),
            dma((2, 2)), dma((2, 2)),
            dma((groups,)), dma((groups,)),
            dma((groups,)), dma((groups,)), dma((groups,)),
            dma((others, per_band // 2)), dma((others, per_band // 2)),
        ],
        compiler_params=pltpu.CompilerParams(
            collective_id=0, has_side_effects=True, vmem_limit_bytes=48 * 1024 * 1024
        ),
    )(
        storm_track, need_tiles, slot_count, background, node_cells, node_fracs,
        elevation.reshape(length, LANES), bed_level.reshape(length, LANES),
    )
    return forcing, surge.reshape(1, -1)


def solution(mesh):
    placed = (
        P(("own", "dom"), None, None),
        P(),
        P(("own", "dom"), None),
        P(("own", "dom"), None),
        P(None, ("own", "dom"), None),
        P(("own", "dom")),
        P("own", "dom"),
        P("own", "dom"),
    )
    return jax.shard_map(
        shards,
        mesh=mesh,
        in_specs=placed,
        out_specs=(P(("own", "dom"), None, None), P("own", "dom")),
        check_vma=False,
    )
```

time: 107 us -> 28.2 us (0.26); the launches traced: 106 us -> 28 us
  other arithmetic: 29 us -> 0 us
  starting transfers between devices: 28.7 us -> 0 us
  Pallas kernels: 0 us -> 24.9 us
  between operations: 18.3 us -> 0.75 us
  waiting for transfers between devices: 15.5 us -> 0 us
  local copies, waits for them, and re-layouts: 11.2 us -> 2.35 us
  matrix products: 2.49 us -> 0 us
    pallas_call x0 -> x1, Pallas kernels: none -> 24.9 us  [shards(): pl.pallas_call(functools.partial(kernel, groups, holders), out_shape=(jax...]
    ppermute x8 -> x0, starting transfers between devices: 21 us -> none  [the longest x4 15.8 us: extended(): lax.ppermute(tail, axis, [(i, (i + 1) % count) for i in range(ends)])]
    unnamed x7 -> x0, other arithmetic: 15.2 us -> none
    all_to_all x2 -> x0, starting transfers between devices: 7.67 us -> none  [the longest x1 4.21 us: shards(): lax.all_to_all(wanted.reshape(groups, K_B), 'own', split_axis=0, concat_a...]
    ppermute x8 -> x0, waiting for transfers between devices: 7.24 us -> none  [the longest x4 7.23 us: extended(): lax.ppermute(head, axis, [((i + 1) % count, i) for i in range(ends)])]
    all_to_all x2 -> x0, waiting for transfers between devices: 7.15 us -> none  [the longest x1 7.14 us: shards(): lax.all_to_all(served.reshape(groups, K_B, FIELDS, cell_count), 'own', sp...]
    another operation x13 -> x0, other arithmetic: 5.49 us -> none  [the longest x1 2.77 us: holland(): jnp.stack(fields, axis=1)]
    dot_general x4 -> x0, matrix products: 2.49 us -> none  [one_block(): jnp.einsum('bkj,bjn->bkn', tile_block, col_weights, preferred_element_typ...]
  transfers between devices with their start and end apart: 11 -> 0, of which waited for: 6 -> 0; matrix products, arithmetic and copies ran while one was open for 9% -> 0% of each run, Pallas kernels for 0% -> 0%
where the time goes in v1:
time: 28.2 us; the launch traced here: 28 us
  Pallas kernels  24.9 us (88%)
  local copies, waits for them, and re-layouts  2.35 us (8%)
  between operations  0.75 us (3%)
    pallas_call x1, Pallas kernels, shards(): pl.pallas_call(functools.partial(kernel, groups, holders), out_shape=(jax...  24.9 us
    unnamed x17, local copies, waits for them, and re-layouts  2.35 us

profile of v1, /device:TPU:0, one launch (start us, length us, event | category | flops | bytes accessed | tf_op | source)
XLA Modules:
  0.0 28.0 jit_solution(7699107570827518605)
XLA Ops:
  0.6 0.0 copy-start
  0.6 0.0 copy-start.1
  0.7 0.0 copy-start.2
  0.7 0.0 copy-start.3
  0.7 0.0 copy-start.4
  0.7 0.0 copy-start.5
  0.7 0.0 copy-start.6
  0.7 1.0 %copy.10.back_ref = bf16[2,6,4096]{2,1,0:T(8,128)(2,1)S(1)} copy(bf16[2,6,4096]{2,0,1:T(2,128)(2,1)} %param.8) | data formatting | bytes 196608 | tf_op args[0]
  1.7 0.0 copy-done
  1.7 0.0 copy-done.1
  1.7 0.0 copy-done.2
  1.7 0.0 copy-done.3
  1.8 0.0 copy-done.4
  1.8 0.0 copy-done.5
  1.8 0.0 copy-done.6
  1.8 24.9 %shard_map.95 = (bf16[8,6,1024]{2,1,0:T(8,128)(2,1)S(1)}, f32[64,128]{1,0:T(8,128)S(1)}) custom-call(f32[2,5]{1,0:T(2,128)S(1)} %copy-done.4, s32[1,8]{1,0:T(1,128)S(1)} %copy-done.5, s32[8]{0:T(128)S(1)} %copy-done.6, bf16[2,6,4096]{2,1,0:T(8,128)(2,1)S(1)} %copy.10.back_ref, s32[8,1024]{1,0:T(8,128)S(1)} %copy-done.1, f32[2,8,1024]{2,1,0:T(8,128)S(1)} %copy-done, ...), custom_call_target="tpu_custom_call" | custom-call | tf_op jit(solution)/shard_map/pallas_call | solution.py:354
  26.7 0.7 %copy.11 = bf16[8,6,1024]{2,0,1:T(8,128)(2,1)} copy(bf16[8,6,1024]{2,1,0:T(8,128)(2,1)S(1)} %get-tuple-element.6) | data formatting | bytes 196608
  27.4 0.6 %copy.13 = f32[1,8192]{1,0:T(1,128)} copy(f32[1,8192]{1,0:T(1,128)S(1)} %bitcast.5) | data formatting | bytes 65536
Async XLA Ops:
  0.6 1.1 %copy-start = (f32[2,8,1024]{2,1,0:T(8,128)S(1)}, f32[2,8,1024]{2,1,0:T(8,128)}, u32[]{:S(2)}) copy-start(f32[2,8,1024]{2,1,0:T(8,128)} %fracs_ref.1) | copy-start | bytes 196612
  0.6 1.1 %copy-start.1 = (s32[8,1024]{1,0:T(8,128)S(1)}, s32[8,1024]{1,0:T(8,128)}, u32[]{:S(2)}) copy-start(s32[8,1024]{1,0:T(8,128)} %cells_ref.1) | copy-start | bytes 98308
  0.7 1.1 %copy-start.2 = (f32[1,8192]{1,0:T(1,128)S(1)}, f32[1,8192]{1,0:T(1,128)}, u32[]{:S(2)}) copy-start(f32[1,8192]{1,0:T(1,128)} %param.14) | copy-start | bytes 98308
  0.7 1.1 %copy-start.3 = (f32[1,8192]{1,0:T(1,128)S(1)}, f32[1,8192]{1,0:T(1,128)}, u32[]{:S(2)}) copy-start(f32[1,8192]{1,0:T(1,128)} %param.15) | copy-start | bytes 98308
  0.7 1.1 %copy-start.4 = (f32[2,5]{1,0:T(2,128)S(1)}, f32[2,5]{1,0:T(2,128)}, u32[]{:S(2)}) copy-start(f32[2,5]{1,0:T(2,128)} %storm_ref.1) | copy-start | bytes 124
  0.7 1.1 %copy-start.5 = (s32[1,8]{1,0:T(1,128)S(1)}, s32[1,8]{1,0:T(1,128)}, u32[]{:S(2)}) copy-start(s32[1,8]{1,0:T(1,128)} %need_ref.1) | copy-start | bytes 100
  0.7 1.1 %copy-start.6 = (s32[8]{0:T(128)S(1)}, s32[8]{0:T(128)}, u32[]{:S(2)}) copy-start(s32[8]{0:T(128)} %count_ref.1) | copy-start | bytes 100

commit v2 on v1

--- a/solution.py
+++ b/solution.py
@@ -20,16 +20,16 @@
     storm_ref, need_ref, count_ref, back_ref, cells_ref, fracs_ref, elev_ref, bed_ref,
     forcing_ref, surge_ref,
     grid_ref, field_ref, data_ref, node_out_ref, need_out_ref, need_in_ref, need_smem,
-    colw_ref, roww_ref, surf_ref, ground_ref, press_ref, res_out_ref, res_in_ref,
+    colw_ref, roww_ref, surf_ref, ground_ref, press_ref, value_ref, res_out_ref, res_in_ref,
     ring_send, ring_recv, sib_send, sib_recv, halo_send, halo_recv,
     node_send, node_recv, need_send, need_recv, need_local, res_send, res_recv,
 ):
     own = lax.axis_index("own")
     dom = lax.axis_index("dom")
-    tiles_dev, fields, cell_count = back_ref.shape
-    slots, positions = cells_ref.shape
+    tiles_dev = grid_ref.shape[0] // holders
+    fields, slots, positions = forcing_ref.shape
+    pairs = grid_ref.shape[1] // fields
     per_band = slots // groups
-    pairs = cell_count // LANES
     chips = holders // 2
     half = chips // 2
     band = tiles_dev * holders
@@ -57,36 +57,30 @@
     for j in range(1, groups):
         pl.semaphore_signal(barrier, inc=1, device_id={"own": (own + j) % groups})
 
-    pair_index = lax.broadcasted_iota(jnp.int32, (pairs, LANES), 0)
-    lane_index = lax.broadcasted_iota(jnp.int32, (pairs, LANES), 1)
-    cell_row = (pair_index * (LANES // TILE) + lane_index // TILE).astype(jnp.float32)
-    cell_col = (lane_index % TILE).astype(jnp.float32)
+    deep = pairs * tiles_dev
+    deep_index = lax.broadcasted_iota(jnp.int32, (deep, LANES), 0)
+    lane_index = lax.broadcasted_iota(jnp.int32, (deep, LANES), 1)
+    tile = own * band + dom * tiles_dev + deep_index % tiles_dev
+    cell_row = deep_index // tiles_dev * (LANES // TILE) + lane_index // TILE
+    north = (tile // TCOLS * TILE + cell_row).astype(jnp.float32)
+    east = (tile % TCOLS * TILE + lane_index % TILE).astype(jnp.float32)
+    for k in range(2):
+        offset_x = east - storm_ref[k, 0]
+        offset_y = north - storm_ref[k, 1]
+        deficit = storm_ref[k, 2]
+        shape = storm_ref[k, 4]
+        radius = jnp.sqrt(offset_x * offset_x + offset_y * offset_y + 1.0)
+        ratio = jnp.exp(shape * jnp.log(storm_ref[k, 3] / radius))
+        decay = jnp.exp(-ratio)
+        speed = jnp.sqrt(shape * deficit * ratio * decay) / radius
+        added = (-speed * offset_y, speed * offset_x, -deficit * (1.0 - decay))
+        for m, term in enumerate(added):
+            rows = pl.ds((3 * k + m) * deep, deep)
+            field_ref[rows, :] = back_ref[rows, :].astype(jnp.float32) + term
     for t in range(tiles_dev):
-        for p in range(pairs):
-            field_ref[pl.ds(p, fields, stride=pairs), :] = back_ref[
-                t, :, p * LANES : (p + 1) * LANES
-            ].astype(jnp.float32)
-        tile = own * band + dom * tiles_dev + t
-        north = (tile // TCOLS * TILE).astype(jnp.float32) + cell_row
-        east = (tile % TCOLS * TILE).astype(jnp.float32) + cell_col
-        mine = grid_ref.at[dom * tiles_dev + t]
-        for k in range(2):
-            offset_x = east - storm_ref[k, 0]
-            offset_y = north - storm_ref[k, 1]
-            deficit = storm_ref[k, 2]
-            shape = storm_ref[k, 4]
-            radius = jnp.sqrt(offset_x * offset_x + offset_y * offset_y + 1.0)
-            ratio = jnp.exp(shape * jnp.log(storm_ref[k, 3] / radius))
-            decay = jnp.exp(-ratio)
-            speed = jnp.sqrt(shape * deficit * ratio * decay)
-            added = (
-                -speed * offset_y / radius,
-                speed * offset_x / radius,
-                -deficit * (1.0 - decay),
-            )
-            for m, term in enumerate(added):
-                rows = pl.ds((3 * k + m) * pairs, pairs)
-                mine[rows, :] = (field_ref[rows, :] + term).astype(jnp.bfloat16)
+        grid_ref[dom * tiles_dev + t] = field_ref[
+            pl.ds(t, fields * pairs, stride=tiles_dev), :
+        ].astype(jnp.bfloat16)
 
     pl.semaphore_wait(barrier, 5 + groups - 1)
 
@@ -245,31 +239,32 @@
             surface = surface - (flux - shifted(flux, 1))
         surf_ref[...] = surface
 
-    work = [functools.partial(weights, 0, i) for i in range(per_band)]
+    own_work = [functools.partial(weights, 0, i) for i in range(per_band)]
+    work = [sweep]
     for j in range(1, groups):
         work.append(functools.partial(await_asked, j))
         work += [functools.partial(weights, j, i) for i in range(per_band)]
-    work.append(sweep)
+    for item in own_work:
+        item()
 
     events = [
-        (way, far, t)
+        [(way, far, t) for way, t in first if far <= reach(way, t)]
         for far in range(1, half + 1)
-        for way, t in first
-        if far <= reach(way, t)
     ]
     done = 0
-    for n, (way, far, t) in enumerate(events):
-        until = (n + 1) * len(work) // len(events)
+    for n, batch in enumerate(events):
+        for way, far, t in batch:
+            ring_arrival(way, far, t).wait_recv()
+            if far < reach(way, t):
+                start(ring_copy(way, far + 1, t))
+            start(sibling_copy(way, far, t, core))
+        until = len(work) if n == half - 1 else (n + 1) * len(work) // max(half - 1, 1)
         for item in work[done:until]:
             item()
-        done = until
-        ring_arrival(way, far, t).wait_recv()
-        if far < reach(way, t):
-            start(ring_copy(way, far + 1, t))
-        start(sibling_copy(way, far, t, core))
+        done = max(done, until)
     for t in range(tiles_dev):
         sibling_copy(0, 0, t, 1 - core).wait_recv()
-    for way, far, t in events:
+    for way, far, t in sum(events, []):
         sibling_copy(way, far, t, 1 - core).wait_recv()
 
     chunk = 256
@@ -290,6 +285,10 @@
                 total = part if total is None else total + part
             parts.append(jnp.sum(total, axis=1))
         return jnp.concatenate(parts, axis=1)
+
+    def keep_forcing(slot, value):
+        for f in range(fields):
+            value_ref[f, pl.ds(slot, 1), :] = value[f : f + 1]
 
     def keep_pressure(slot, pressure):
         for m in range(positions // LANES):
@@ -317,18 +316,18 @@
     for i in range(per_band):
         slot = own * per_band + i
         value = node_values(0, i, need_ref[0, slot])
-        forcing_ref[slot] = value.astype(jnp.bfloat16)
+        keep_forcing(slot, value)
         keep_pressure(slot, value[fields - 1 : fields])
     for j, m, copy in answers:
         copy.wait_recv()
         got = res_in_ref[j - 1, m].astype(jnp.float32)
         for i in range(2):
             slot = (own + j) % groups * per_band + 2 * m + i
-            value = got[8 * i : 8 * i + fields]
-            forcing_ref[slot] = value.astype(jnp.bfloat16)
+            keep_forcing(slot, got[8 * i : 8 * i + fields])
             keep_pressure(
                 slot, got[8 * i + fields - 1 : 8 * i + fields] + got[8 * i + fields : 8 * i + fields + 1]
             )
+    forcing_ref[...] = value_ref[...].astype(jnp.bfloat16)
     surface = surf_ref[pl.ds(HALO, length), :]
     surge_ref[...] = surface - 0.5 * press_ref[...] * jnp.clip(surface - bed_ref[...], 0.0, 1.0)
     for copy in sent:
@@ -354,14 +353,14 @@
     forcing, surge = pl.pallas_call(
         functools.partial(kernel, groups, holders),
         out_shape=(
-            jax.ShapeDtypeStruct((slots, fields, positions), jnp.bfloat16),
+            jax.ShapeDtypeStruct((fields, slots, positions), jnp.bfloat16),
             jax.ShapeDtypeStruct((length, LANES), jnp.float32),
         ),
         in_specs=[smem] * 3 + [vmem] * 5,
         out_specs=(vmem, vmem),
         scratch_shapes=[
             pltpu.VMEM((tiles_dev * holders, fields * pairs, LANES), jnp.bfloat16),
-            pltpu.VMEM((fields * pairs, LANES), jnp.float32),
+            pltpu.VMEM((fields * pairs * tiles_dev, LANES), jnp.float32),
             pltpu.VMEM((groups, 4 * per_band, positions), jnp.float32),
             pltpu.VMEM((others, 4 * per_band, positions), jnp.float32),
             pltpu.VMEM((others, 8, LANES), jnp.int32),
@@ -372,6 +371,7 @@
             pltpu.VMEM((length + 2 * HALO, LANES), jnp.float32),
             pltpu.VMEM((length + 2 * HALO, LANES), jnp.float32),
             pltpu.VMEM((length, LANES), jnp.float32),
+            pltpu.VMEM((fields, slots, positions), jnp.float32),
             pltpu.VMEM((others, per_band // 2, 16, positions), jnp.bfloat16),
             pltpu.VMEM((others, per_band // 2, 16, positions), jnp.bfloat16),
             dma((2, half, tiles_dev)), dma((2, half, tiles_dev)),
@@ -385,10 +385,14 @@
             collective_id=0, has_side_effects=True, vmem_limit_bytes=48 * 1024 * 1024
         ),
     )(
-        storm_track, need_tiles, slot_count, background, node_cells, node_fracs,
+        storm_track, need_tiles, slot_count,
+        background.reshape(tiles_dev, fields, pairs, LANES)
+        .transpose(1, 2, 0, 3)
+        .reshape(fields * pairs * tiles_dev, LANES),
+        node_cells, node_fracs,
         elevation.reshape(length, LANES), bed_level.reshape(length, LANES),
     )
-    return forcing, surge.reshape(1, -1)
+    return forcing.transpose(1, 0, 2), surge.reshape(1, -1)
 
 
 def solution(mesh):

time: 28.2 us -> 31.9 us (1.13)
  local copies, waits for them, and re-layouts: 2.35 us -> 5.93 us
    unnamed x17 -> x18, local copies, waits for them, and re-layouts: 2.35 us -> 5.93 us
where the time goes in v2:
time: 31.9 us; the launch traced here: 31.5 us
  Pallas kernels  24.9 us (78%)
  local copies, waits for them, and re-layouts  5.93 us (19%)
  between operations  0.67 us (2%)
    pallas_call x1, Pallas kernels, shards(): pl.pallas_call(functools.partial(kernel, groups, holders), out_shape=(jax...  24.9 us
    unnamed x18, local copies, waits for them, and re-layouts  5.93 us

profile of v2, /device:TPU:0, one launch (start us, length us, event | category | flops | bytes accessed | tf_op | source)
XLA Modules:
  0.0 31.5 jit_solution(16701278065091804198)
XLA Ops:
  0.6 0.0 copy-start.7
  0.6 0.0 copy-start.5
  0.7 0.0 copy-start.6
  0.7 0.6 %copy-done.7 = s32[8]{0:T(128)S(1)} copy-done((s32[8]{0:T(128)S(1)}, s32[8]{0:T(128)}, u32[]{:S(2)}) %copy-start.7) | copy-done | bytes 56
  1.3 0.0 copy-done.5
  1.3 0.0 copy-done.6
  1.3 0.0 copy-start
  1.3 0.9 %copy-done = bf16[2,6,4096]{2,0,1:T(2,128)(2,1)S(1)} copy-done((bf16[2,6,4096]{2,0,1:T(2,128)(2,1)S(1)}, bf16[2,6,4096]{2,0,1:T(2,128)(2,1)}, u32[]{:S(2)}) %copy-start) | copy-done | bytes 98328
  2.2 0.0 copy-start.1
  2.2 0.8 %copy-done.1 = f32[2,8,1024]{2,1,0:T(8,128)S(1)} copy-done((f32[2,8,1024]{2,1,0:T(8,128)S(1)}, f32[2,8,1024]{2,1,0:T(8,128)}, u32[]{:S(2)}) %copy-start.1) | copy-done | bytes 65560
  3.1 0.0 copy-start.2
  3.1 0.8 %copy-done.2 = s32[8,1024]{1,0:T(8,128)S(1)} copy-done((s32[8,1024]{1,0:T(8,128)S(1)}, s32[8,1024]{1,0:T(8,128)}, u32[]{:S(2)}) %copy-start.2) | copy-done | bytes 32792
  3.8 0.0 copy-start.3
  3.8 0.8 %copy-done.3 = f32[1,8192]{1,0:T(1,128)S(1)} copy-done((f32[1,8192]{1,0:T(1,128)S(1)}, f32[1,8192]{1,0:T(1,128)}, u32[]{:S(2)}) %copy-start.3) | copy-done | bytes 32792
  4.6 0.0 copy-start.4
  4.6 0.8 %copy-done.4 = f32[1,8192]{1,0:T(1,128)S(1)} copy-done((f32[1,8192]{1,0:T(1,128)S(1)}, f32[1,8192]{1,0:T(1,128)}, u32[]{:S(2)}) %copy-start.4) | copy-done | bytes 32792
  5.3 24.9 %shard_map.95 = (bf16[6,8,1024]{2,1,0:T(8,128)(2,1)S(1)}, f32[64,128]{1,0:T(8,128)S(1)}) custom-call(f32[2,5]{1,0:T(2,128)S(1)} %copy-done.5, s32[1,8]{1,0:T(1,128)S(1)} %copy-done.6, s32[8]{0:T(128)S(1)} %copy-done.7, bf16[384,128]{1,0:T(8,128)(2,1)S(1)} %bitcast.9, s32[8,1024]{1,0:T(8,128)S(1)} %copy-done.2, f32[2,8,1024]{2,1,0:T(8,128)S(1)} %copy-done.1, ...), custom_call_target="tpu_custom_call" | custom-call | tf_op jit(solution)/shard_map/pallas_call | solution.py:353
  30.2 0.6 %copy.13 = bf16[8,6,1024]{2,0,1:T(8,128)(2,1)} copy(bf16[8,6,1024]{2,0,1:T(8,128)(2,1)S(1)} %bitcast.10) | data formatting | bytes 196608
  30.9 0.6 %copy.14 = f32[1,8192]{1,0:T(1,128)} copy(f32[1,8192]{1,0:T(1,128)S(1)} %bitcast.11) | data formatting | bytes 65536
Async XLA Ops:
  0.6 0.7 %copy-start.7 = (s32[8]{0:T(128)S(1)}, s32[8]{0:T(128)}, u32[]{:S(2)}) copy-start(s32[8]{0:T(128)} %count_ref.1) | copy-start | bytes 100
  0.6 0.7 %copy-start.5 = (f32[2,5]{1,0:T(2,128)S(1)}, f32[2,5]{1,0:T(2,128)}, u32[]{:S(2)}) copy-start(f32[2,5]{1,0:T(2,128)} %storm_ref.1) | copy-start | bytes 124
  0.7 0.7 %copy-start.6 = (s32[1,8]{1,0:T(1,128)S(1)}, s32[1,8]{1,0:T(1,128)}, u32[]{:S(2)}) copy-start(s32[1,8]{1,0:T(1,128)} %need_ref.1) | copy-start | bytes 100
  1.3 0.9 %copy-start = (bf16[2,6,4096]{2,0,1:T(2,128)(2,1)S(1)}, bf16[2,6,4096]{2,0,1:T(2,128)(2,1)}, u32[]{:S(2)}) copy-start(bf16[2,6,4096]{2,0,1:T(2,128)(2,1)} %param.8) | copy-start | bytes 294916
  2.2 0.8 %copy-start.1 = (f32[2,8,1024]{2,1,0:T(8,128)S(1)}, f32[2,8,1024]{2,1,0:T(8,128)}, u32[]{:S(2)}) copy-start(f32[2,8,1024]{2,1,0:T(8,128)} %fracs_ref.1) | copy-start | bytes 196612
  3.1 0.8 %copy-start.2 = (s32[8,1024]{1,0:T(8,128)S(1)}, s32[8,1024]{1,0:T(8,128)}, u32[]{:S(2)}) copy-start(s32[8,1024]{1,0:T(8,128)} %cells_ref.1) | copy-start | bytes 98308
  3.8 0.8 %copy-start.3 = (f32[1,8192]{1,0:T(1,128)S(1)}, f32[1,8192]{1,0:T(1,128)}, u32[]{:S(2)}) copy-start(f32[1,8192]{1,0:T(1,128)} %param.14) | copy-start | bytes 98308
  4.6 0.8 %copy-start.4 = (f32[1,8192]{1,0:T(1,128)S(1)}, f32[1,8192]{1,0:T(1,128)}, u32[]{:S(2)}) copy-start(f32[1,8192]{1,0:T(1,128)} %param.15) | copy-start | bytes 98308

commit v3 on v2

--- a/solution.py
+++ b/solution.py
@@ -17,8 +17,9 @@
 
 def kernel(
     groups, holders,
-    storm_ref, need_ref, count_ref, back_ref, cells_ref, fracs_ref, elev_ref, bed_ref,
+    storm_hbm, need_hbm, count_hbm, back_hbm, cells_hbm, fracs_hbm, elev_ref, bed_ref,
     forcing_ref, surge_ref,
+    storm_ref, need_ref, count_ref, back_ref, cells_ref, fracs_ref, fetch_sem,
     grid_ref, field_ref, data_ref, node_out_ref, need_out_ref, need_in_ref, need_smem,
     colw_ref, roww_ref, surf_ref, ground_ref, press_ref, value_ref, res_out_ref, res_in_ref,
     ring_send, ring_recv, sib_send, sib_recv, halo_send, halo_recv,
@@ -51,6 +52,19 @@
     after = (dom + 1) % holders
     before = (dom + holders - 1) % holders
 
+    length = elev_ref.shape[0]
+    inner = pl.ds(HALO, length)
+    fetched = [
+        pltpu.make_async_copy(source, target, fetch_sem.at[n])
+        for n, (source, target) in enumerate((
+            (back_hbm, back_ref), (storm_hbm, storm_ref), (need_hbm, need_ref),
+            (count_hbm, count_ref), (cells_hbm, cells_ref), (fracs_hbm, fracs_ref),
+            (elev_ref, surf_ref.at[inner]), (bed_ref, ground_ref.at[inner]),
+        ))
+    ]
+    for copy in fetched:
+        copy.start()
+
     barrier = pltpu.get_barrier_semaphore()
     for neighbour in (right, left, sibling, after, before):
         pl.semaphore_signal(barrier, inc=1, device_id={"dom": neighbour})
@@ -64,6 +78,8 @@
     cell_row = deep_index // tiles_dev * (LANES // TILE) + lane_index // TILE
     north = (tile // TCOLS * TILE + cell_row).astype(jnp.float32)
     east = (tile % TCOLS * TILE + lane_index % TILE).astype(jnp.float32)
+    for copy in fetched[:2]:
+        copy.wait()
     for k in range(2):
         offset_x = east - storm_ref[k, 0]
         offset_y = north - storm_ref[k, 1]
@@ -130,7 +146,6 @@
     for t in range(tiles_dev):
         start(sibling_copy(0, 0, t, core))
 
-    length = elev_ref.shape[0]
     ends = ((after, length - HALO, 0, 0), (before, 0, HALO + length, 1))
     halo = []
     for target, source_row, target_row, side in ends:
@@ -151,13 +166,15 @@
         group = (own + j) % groups
         for i in range(per_band):
             slot = group * per_band + i
-            live = live_index < count_ref[slot]
+            live = live_index < count_ref[0, slot]
             north_frac = fracs_ref[1, pl.ds(slot, 1), :]
             target[pl.ds(i, 1), :] = cells_ref[pl.ds(slot, 1), :].astype(jnp.float32)
             target[pl.ds(per_band + i, 1), :] = fracs_ref[0, pl.ds(slot, 1), :]
             target[pl.ds(2 * per_band + i, 1), :] = jnp.where(live, 1.0 - north_frac, 0.0)
             target[pl.ds(3 * per_band + i, 1), :] = jnp.where(live, north_frac, 0.0)
 
+    for copy in fetched[2:6]:
+        copy.wait()
     asked = []
     for j in range(1, groups):
         group = (own + j) % groups
@@ -212,8 +229,8 @@
         local.wait()
 
     def sweep():
-        surf_ref[pl.ds(HALO, length), :] = elev_ref[...]
-        ground_ref[pl.ds(HALO, length), :] = bed_ref[...]
+        for copy in fetched[6:]:
+            copy.wait()
         for copy in halo:
             copy.wait_recv()
         surface = surf_ref[...]
@@ -328,8 +345,10 @@
                 slot, got[8 * i + fields - 1 : 8 * i + fields] + got[8 * i + fields : 8 * i + fields + 1]
             )
     forcing_ref[...] = value_ref[...].astype(jnp.bfloat16)
-    surface = surf_ref[pl.ds(HALO, length), :]
-    surge_ref[...] = surface - 0.5 * press_ref[...] * jnp.clip(surface - bed_ref[...], 0.0, 1.0)
+    surface = surf_ref[inner, :]
+    surge_ref[...] = surface - 0.5 * press_ref[...] * jnp.clip(
+        surface - ground_ref[inner, :], 0.0, 1.0
+    )
     for copy in sent:
         copy.wait_send()
 
@@ -348,7 +367,7 @@
     length = elevation.shape[1] // LANES
     others = max(groups - 1, 1)
     vmem = pl.BlockSpec(memory_space=pltpu.VMEM)
-    smem = pl.BlockSpec(memory_space=pltpu.SMEM)
+    hbm = pl.BlockSpec(memory_space=pltpu.HBM)
     dma = pltpu.SemaphoreType.DMA
     forcing, surge = pl.pallas_call(
         functools.partial(kernel, groups, holders),
@@ -356,9 +375,16 @@
             jax.ShapeDtypeStruct((fields, slots, positions), jnp.bfloat16),
             jax.ShapeDtypeStruct((length, LANES), jnp.float32),
         ),
-        in_specs=[smem] * 3 + [vmem] * 5,
+        in_specs=[hbm] * 8,
         out_specs=(vmem, vmem),
         scratch_shapes=[
+            pltpu.SMEM(storm_track.shape, jnp.float32),
+            pltpu.SMEM((1, slots), jnp.int32),
+            pltpu.SMEM((1, slots), jnp.int32),
+            pltpu.VMEM((fields * pairs * tiles_dev, LANES), jnp.bfloat16),
+            pltpu.VMEM((slots, positions), jnp.int32),
+            pltpu.VMEM((2, slots, positions), jnp.float32),
+            dma((8,)),
             pltpu.VMEM((tiles_dev * holders, fields * pairs, LANES), jnp.bfloat16),
             pltpu.VMEM((fields * pairs * tiles_dev, LANES), jnp.float32),
             pltpu.VMEM((groups, 4 * per_band, positions), jnp.float32),
@@ -382,10 +408,10 @@
             dma((others, per_band // 2)), dma((others, per_band // 2)),
         ],
         compiler_params=pltpu.CompilerParams(
-            collective_id=0, has_side_effects=True, vmem_limit_bytes=48 * 1024 * 1024
+            collective_id=0, has_side_effects=True, vmem_limit_bytes=60 * 1024 * 1024
         ),
     )(
-        storm_track, need_tiles, slot_count,
+        storm_track, need_tiles, slot_count.reshape(1, slots),
         background.reshape(tiles_dev, fields, pairs, LANES)
         .transpose(1, 2, 0, 3)
         .reshape(fields * pairs * tiles_dev, LANES),

time: 31.9 us -> 28.1 us (0.88)
  local copies, waits for them, and re-layouts: 5.93 us -> 2.16 us
    unnamed x18 -> x4, local copies, waits for them, and re-layouts: 5.93 us -> 2.16 us
where the time goes in v3:
time: 28.1 us; the launch traced here: 28 us
  Pallas kernels  25.2 us (90%)
  local copies, waits for them, and re-layouts  2.16 us (8%)
  between operations  0.65 us (2%)
    pallas_call x1, Pallas kernels, shards(): pl.pallas_call(functools.partial(kernel, groups, holders), out_shape=(jax...  25.2 us
    unnamed x4, local copies, waits for them, and re-layouts  2.16 us

profile of v3, /device:TPU:0, one launch (start us, length us, event | category | flops | bytes accessed | tf_op | source)
XLA Modules:
  0.0 28.0 jit_solution(14760485500644998636)
XLA Ops:
  0.6 25.2 %shard_map.95 = (bf16[6,8,1024]{2,1,0:T(8,128)(2,1)}, f32[64,128]{1,0:T(8,128)}) custom-call(f32[2,5]{1,0:T(2,128)} %storm_hbm.1, s32[1,8]{1,0:T(1,128)} %need_hbm.1, s32[1,8]{1,0:T(1,128)} %bitcast.15, bf16[384,128]{1,0:T(8,128)(2,1)} %bitcast.10, s32[8,1024]{1,0:T(8,128)} %cells_hbm.1, f32[2,8,1024]{2,1,0:T(8,128)} %fracs_hbm.1, f32[64,128]{1,0:T(8,128)} %bitcast.13, ...), custom_call_target="tpu_custom_call" | custom-call | tf_op jit(solution)/shard_map/pallas_call | solution.py:372
  25.8 0.0 copy-start
  25.8 1.5 %copy.13 = bf16[8,6,1024]{2,0,1:T(8,128)(2,1)} copy(bf16[8,6,1024]{2,0,1:T(8,128)(2,1)} %bitcast.11) | data formatting | bytes 196608
  27.3 0.0 copy-done
  27.3 0.6 %copy.14 = f32[1,8192]{1,0:T(1,128)} copy(f32[1,8192]{1,0:T(1,128)S(1)} %bitcast.12) | data formatting | bytes 65536
Async XLA Ops:
  25.8 1.6 %copy-start = (f32[64,128]{1,0:T(8,128)S(1)}, f32[64,128]{1,0:T(8,128)}, u32[]{:S(2)}) copy-start(f32[64,128]{1,0:T(8,128)} %get-tuple-element.5) | copy-start | bytes 98308

commit v4 on v3

--- a/solution.py
+++ b/solution.py
@@ -139,12 +139,15 @@
         copy.start()
         sent.append(copy)
 
-    first = [(way, (way + s) % tiles_dev) for s in range(tiles_dev) for way in range(2)]
-    for way, t in first:
-        if reach(way, t) >= 1:
-            start(ring_copy(way, 1, t))
-    for t in range(tiles_dev):
-        start(sibling_copy(0, 0, t, core))
+    waves = [[(way, (way + s) % tiles_dev) for way in range(2)] for s in range(tiles_dev)]
+
+    def begin(wave):
+        copies = [ring_copy(way, 1, t) for way, t in wave if reach(way, t) >= 1]
+        for copy in copies:
+            copy.start()
+        return copies
+
+    started = begin(waves[0])
 
     ends = ((after, length - HALO, 0, 0), (before, 0, HALO + length, 1))
     halo = []
@@ -196,8 +199,6 @@
         )
         start(need)
         asked.append((node, need))
-    node_rows(0, data_ref.at[0])
-
     col_index = lax.broadcasted_iota(jnp.int32, (TILE, positions), 0)
     even_index = lax.broadcasted_iota(jnp.int32, (pairs, positions), 0) * 2
 
@@ -218,6 +219,18 @@
                 row == row_first, upper, jnp.where(row == row_first + 1, lower, 0.0)
             )
 
+    for n, wave in enumerate(waves):
+        for copy in started:
+            copy.wait_send()
+        if n + 1 < tiles_dev:
+            started = begin(waves[n + 1])
+        if n == 0:
+            for t in range(tiles_dev):
+                start(sibling_copy(0, 0, t, core))
+            node_rows(0, data_ref.at[0])
+            for i in range(per_band // 2):
+                weights(0, i)
+
     def await_asked(j):
         node, need = asked[j - 1]
         need.wait_recv()
@@ -256,29 +269,30 @@
             surface = surface - (flux - shifted(flux, 1))
         surf_ref[...] = surface
 
-    own_work = [functools.partial(weights, 0, i) for i in range(per_band)]
-    work = [sweep]
+    work = [functools.partial(weights, 0, i) for i in range(per_band // 2, per_band)]
+    work.append(sweep)
     for j in range(1, groups):
         work.append(functools.partial(await_asked, j))
         work += [functools.partial(weights, j, i) for i in range(per_band)]
-    for item in own_work:
-        item()
 
     events = [
-        [(way, far, t) for way, t in first if far <= reach(way, t)]
+        [(way, far, t) for way, t in wave if far <= reach(way, t)]
         for far in range(1, half + 1)
+        for wave in waves
     ]
+    events = [batch for batch in events if batch]
     done = 0
     for n, batch in enumerate(events):
         for way, far, t in batch:
             ring_arrival(way, far, t).wait_recv()
             if far < reach(way, t):
                 start(ring_copy(way, far + 1, t))
+        for way, far, t in batch:
             start(sibling_copy(way, far, t, core))
-        until = len(work) if n == half - 1 else (n + 1) * len(work) // max(half - 1, 1)
+        until = (n + 1) * len(work) // max(len(events) - 1, 1) if n + 1 < len(events) else len(work)
         for item in work[done:until]:
             item()
-        done = max(done, until)
+        done = until
     for t in range(tiles_dev):
         sibling_copy(0, 0, t, 1 - core).wait_recv()
     for way, far, t in sum(events, []):
@@ -351,6 +365,17 @@
     )
     for copy in sent:
         copy.wait_send()
+
+
+def hand_over(forcing_in, surge_in, forcing_out, surge_out, sem):
+    copies = [
+        pltpu.make_async_copy(forcing_in, forcing_out, sem.at[0]),
+        pltpu.make_async_copy(surge_in, surge_out, sem.at[1]),
+    ]
+    for copy in copies:
+        copy.start()
+    for copy in copies:
+        copy.wait()
 
 
 def shards(
@@ -418,6 +443,17 @@
         node_cells, node_fracs,
         elevation.reshape(length, LANES), bed_level.reshape(length, LANES),
     )
+    forcing, surge = pl.pallas_call(
+        hand_over,
+        out_shape=(
+            jax.ShapeDtypeStruct(forcing.shape, forcing.dtype),
+            jax.ShapeDtypeStruct(surge.shape, surge.dtype),
+        ),
+        in_specs=[hbm] * 2,
+        out_specs=(hbm, hbm),
+        scratch_shapes=[dma((2,))],
+        compiler_params=pltpu.CompilerParams(vmem_limit_bytes=60 * 1024 * 1024),
+    )(forcing, surge)
     return forcing.transpose(1, 0, 2), surge.reshape(1, -1)
 
 

time: 28.1 us -> 30.8 us (1.096)
  Pallas kernels: 25.2 us -> 30 us
  local copies, waits for them, and re-layouts: 2.16 us -> 0 us
    pallas_call x0 -> x1, Pallas kernels: none -> 5.09 us  [shards(): pl.pallas_call(hand_over, out_shape=(jax.ShapeDtypeStruct(forcing.shape,...]
    unnamed x4 -> x0, local copies, waits for them, and re-layouts: 2.16 us -> none
where the time goes in v4:
time: 30.8 us; the launch traced here: 30.7 us
  Pallas kernels  30 us (97%)
  between operations  0.64 us (2%)
    pallas_call x1, Pallas kernels, shards(): pl.pallas_call(functools.partial(kernel, groups, holders), out_shape=(jax...  25 us
    pallas_call x1, Pallas kernels, shards(): pl.pallas_call(hand_over, out_shape=(jax.ShapeDtypeStruct(forcing.shape,...  5.09 us

profile of v4, /device:TPU:0, one launch (start us, length us, event | category | flops | bytes accessed | tf_op | source)
XLA Modules:
  0.0 30.7 jit_solution(3648210317412652808)
XLA Ops:
  0.6 25.0 %shard_map.95 = (bf16[6,8,1024]{2,1,0:T(8,128)(2,1)}, f32[64,128]{1,0:T(8,128)}) custom-call(f32[2,5]{1,0:T(2,128)} %storm_hbm.1, s32[1,8]{1,0:T(1,128)} %need_hbm.1, s32[1,8]{1,0:T(1,128)} %bitcast.13, bf16[384,128]{1,0:T(8,128)(2,1)} %bitcast.10, s32[8,1024]{1,0:T(8,128)} %cells_hbm.1, f32[2,8,1024]{2,1,0:T(8,128)} %fracs_hbm.1, f32[64,128]{1,0:T(8,128)} %bitcast.11, ...), custom_call_target="tpu_custom_call" | custom-call | tf_op jit(solution)/shard_map/pallas_call | solution.py:397
  25.6 5.1 %shard_map.96 = (bf16[6,8,1024]{2,1,0:T(8,128)(2,1)}, f32[64,128]{1,0:T(8,128)}) custom-call(bf16[6,8,1024]{2,1,0:T(8,128)(2,1)} %get-tuple-element.6.forcing_in, f32[64,128]{1,0:T(8,128)} %get-tuple-element.7.surge_in), custom_call_target="tpu_custom_call" | custom-call | tf_op jit(solution)/shard_map/pallas_call | solution.py:446

commit v5 on v4

--- a/solution.py
+++ b/solution.py
@@ -167,7 +167,8 @@
 
     def node_rows(j, target):
         group = (own + j) % groups
-        for i in range(per_band):
+        @pl.loop(0, per_band)
+        def _(i):
             slot = group * per_band + i
             live = live_index < count_ref[0, slot]
             north_frac = fracs_ref[1, pl.ds(slot, 1), :]
@@ -219,6 +220,11 @@
                 row == row_first, upper, jnp.where(row == row_first + 1, lower, 0.0)
             )
 
+    def group_weights(j):
+        @pl.loop(0, per_band)
+        def _(i):
+            weights(j, i)
+
     for n, wave in enumerate(waves):
         for copy in started:
             copy.wait_send()
@@ -228,8 +234,7 @@
             for t in range(tiles_dev):
                 start(sibling_copy(0, 0, t, core))
             node_rows(0, data_ref.at[0])
-            for i in range(per_band // 2):
-                weights(0, i)
+            group_weights(0)
 
     def await_asked(j):
         node, need = asked[j - 1]
@@ -269,11 +274,10 @@
             surface = surface - (flux - shifted(flux, 1))
         surf_ref[...] = surface
 
-    work = [functools.partial(weights, 0, i) for i in range(per_band // 2, per_band)]
-    work.append(sweep)
+    work = [sweep]
     for j in range(1, groups):
         work.append(functools.partial(await_asked, j))
-        work += [functools.partial(weights, j, i) for i in range(per_band)]
+        work.append(functools.partial(group_weights, j))
 
     events = [
         [(way, far, t) for way, t in wave if far <= reach(way, t)]
@@ -289,7 +293,7 @@
                 start(ring_copy(way, far + 1, t))
         for way, far, t in batch:
             start(sibling_copy(way, far, t, core))
-        until = (n + 1) * len(work) // max(len(events) - 1, 1) if n + 1 < len(events) else len(work)
+        until = min(n, len(work)) if n + 1 < len(events) else len(work)
         for item in work[done:until]:
             item()
         done = until
@@ -327,37 +331,45 @@
                 :, m * LANES : (m + 1) * LANES
             ]
 
-    answers = []
-    for j in range(1, groups):
-        for m in range(per_band // 2):
+    def answer(j, m):
+        return pltpu.make_async_remote_copy(
+            src_ref=res_out_ref.at[j - 1, m], dst_ref=res_in_ref.at[j - 1, m],
+            send_sem=res_send.at[j - 1, m], recv_sem=res_recv.at[j - 1, m],
+            device_id={"own": (own + groups - j) % groups},
+        )
+
+    for j in range(1, groups):
+
+        @pl.loop(0, per_band // 2)
+        def _(m):
             rows = []
-            for i in (2 * m, 2 * m + 1):
-                value = node_values(j, i, need_smem[j - 1, i, 0])
+            for i in range(2):
+                value = node_values(j, 2 * m + i, need_smem[j - 1, 2 * m + i, 0])
                 pressure = value[fields - 1 : fields]
                 rest = pressure - pressure.astype(jnp.bfloat16).astype(jnp.float32)
                 rows += [value, rest, jnp.zeros((8 - fields - 1, positions), jnp.float32)]
             res_out_ref[j - 1, m] = jnp.concatenate(rows, axis=0).astype(jnp.bfloat16)
-            copy = pltpu.make_async_remote_copy(
-                src_ref=res_out_ref.at[j - 1, m], dst_ref=res_in_ref.at[j - 1, m],
-                send_sem=res_send.at[j - 1, m], recv_sem=res_recv.at[j - 1, m],
-                device_id={"own": (own + groups - j) % groups},
-            )
-            start(copy)
-            answers.append((j, m, copy))
-    for i in range(per_band):
+            answer(j, m).start()
+
+    @pl.loop(0, per_band)
+    def _(i):
         slot = own * per_band + i
         value = node_values(0, i, need_ref[0, slot])
         keep_forcing(slot, value)
         keep_pressure(slot, value[fields - 1 : fields])
-    for j, m, copy in answers:
-        copy.wait_recv()
-        got = res_in_ref[j - 1, m].astype(jnp.float32)
-        for i in range(2):
-            slot = (own + j) % groups * per_band + 2 * m + i
-            keep_forcing(slot, got[8 * i : 8 * i + fields])
-            keep_pressure(
-                slot, got[8 * i + fields - 1 : 8 * i + fields] + got[8 * i + fields : 8 * i + fields + 1]
-            )
+
+    for j in range(1, groups):
+
+        @pl.loop(0, per_band // 2)
+        def _(m):
+            answer(j, m).wait_recv()
+            got = res_in_ref[j - 1, m].astype(jnp.float32)
+            for i in range(2):
+                slot = (own + j) % groups * per_band + 2 * m + i
+                value = got[8 * i : 8 * i + fields]
+                keep_forcing(slot, value)
+                keep_pressure(slot, value[fields - 1 :] + got[8 * i + fields : 8 * i + fields + 1])
+
     forcing_ref[...] = value_ref[...].astype(jnp.bfloat16)
     surface = surf_ref[inner, :]
     surge_ref[...] = surface - 0.5 * press_ref[...] * jnp.clip(
@@ -365,6 +377,9 @@
     )
     for copy in sent:
         copy.wait_send()
+    for j in range(1, groups):
+        for m in range(per_band // 2):
+            answer(j, m).wait_send()
 
 
 def hand_over(forcing_in, surge_in, forcing_out, surge_out, sem):
@@ -397,8 +412,8 @@
     forcing, surge = pl.pallas_call(
         functools.partial(kernel, groups, holders),
         out_shape=(
-            jax.ShapeDtypeStruct((fields, slots, positions), jnp.bfloat16),
-            jax.ShapeDtypeStruct((length, LANES), jnp.float32),
+            pltpu.VMEM((fields, slots, positions), jnp.bfloat16),
+            pltpu.VMEM((length, LANES), jnp.float32),
         ),
         in_specs=[hbm] * 8,
         out_specs=(vmem, vmem),
@@ -449,10 +464,9 @@
             jax.ShapeDtypeStruct(forcing.shape, forcing.dtype),
             jax.ShapeDtypeStruct(surge.shape, surge.dtype),
         ),
-        in_specs=[hbm] * 2,
+        in_specs=[vmem] * 2,
         out_specs=(hbm, hbm),
         scratch_shapes=[dma((2,))],
-        compiler_params=pltpu.CompilerParams(vmem_limit_bytes=60 * 1024 * 1024),
     )(forcing, surge)
     return forcing.transpose(1, 0, 2), surge.reshape(1, -1)
 

time: 30.8 us -> 27.9 us (0.906)
  Pallas kernels: 30 us -> 25.9 us
  local copies, waits for them, and re-layouts: 0 us -> 1.23 us
    pallas_call x1, Pallas kernels: 5.09 us -> 1.56 us  [shards(): pl.pallas_call(hand_over, out_shape=(jax.ShapeDtypeStruct(forcing.shape,...]
    unnamed x0 -> x4, local copies, waits for them, and re-layouts: none -> 1.23 us
    pallas_call x1, Pallas kernels: 25 us -> 24.3 us  [shards(): pl.pallas_call(functools.partial(kernel, groups, holders), out_shape=(plt...]
where the time goes in v5:
time: 27.9 us; the launch traced here: 27.8 us
  Pallas kernels  25.9 us (93%)
  local copies, waits for them, and re-layouts  1.23 us (4%)
  between operations  0.65 us (2%)
    pallas_call x1, Pallas kernels, shards(): pl.pallas_call(functools.partial(kernel, groups, holders), out_shape=(plt...  24.3 us
    pallas_call x1, Pallas kernels, shards(): pl.pallas_call(hand_over, out_shape=(jax.ShapeDtypeStruct(forcing.shape,...  1.56 us
    unnamed x4, local copies, waits for them, and re-layouts  1.23 us

profile of v5, /device:TPU:0, one launch (start us, length us, event | category | flops | bytes accessed | tf_op | source)
XLA Modules:
  0.0 27.8 jit_solution(701284797359713368)
XLA Ops:
  0.6 24.3 %shard_map.95 = (bf16[6,8,1024]{2,1,0:T(8,128)(2,1)S(1)}, f32[64,128]{1,0:T(8,128)S(1)}) custom-call(f32[2,5]{1,0:T(2,128)} %storm_hbm.1, s32[1,8]{1,0:T(1,128)} %need_hbm.1, s32[1,8]{1,0:T(1,128)} %bitcast.13, bf16[384,128]{1,0:T(8,128)(2,1)} %bitcast.10, s32[8,1024]{1,0:T(8,128)} %cells_hbm.1, f32[2,8,1024]{2,1,0:T(8,128)} %fracs_hbm.1, ...), custom_call_target="tpu_custom_call" | custom-call | tf_op jit(solution)/shard_map/pallas_call | solution.py:412
  25.0 0.0 copy-start
  25.0 0.6 %copy-done = bf16[6,8,1024]{2,1,0:T(8,128)(2,1)} copy-done((bf16[6,8,1024]{2,1,0:T(8,128)(2,1)}, bf16[6,8,1024]{2,1,0:T(8,128)(2,1)S(1)}, u32[]{:S(2)}) %copy-start) | copy-done | bytes 98328
  25.6 0.0 copy-start.1
  25.6 0.6 %copy-done.1 = f32[64,128]{1,0:T(8,128)} copy-done((f32[64,128]{1,0:T(8,128)}, f32[64,128]{1,0:T(8,128)S(1)}, u32[]{:S(2)}) %copy-start.1) | copy-done | bytes 32792
  26.2 1.6 %shard_map.96 = (bf16[6,8,1024]{2,1,0:T(8,128)(2,1)}, f32[64,128]{1,0:T(8,128)}) custom-call(bf16[6,8,1024]{2,1,0:T(8,128)(2,1)} %copy-done, f32[64,128]{1,0:T(8,128)} %copy-done.1), custom_call_target="tpu_custom_call" | custom-call | tf_op jit(solution)/shard_map/pallas_call | solution.py:461
Async XLA Ops:
  25.0 0.6 %copy-start = (bf16[6,8,1024]{2,1,0:T(8,128)(2,1)}, bf16[6,8,1024]{2,1,0:T(8,128)(2,1)S(1)}, u32[]{:S(2)}) copy-start(bf16[6,8,1024]{2,1,0:T(8,128)(2,1)S(1)} %get-tuple-element.6.forcing_in) | copy-start | bytes 294916
  25.6 0.6 %copy-start.1 = (f32[64,128]{1,0:T(8,128)}, f32[64,128]{1,0:T(8,128)S(1)}, u32[]{:S(2)}) copy-start(f32[64,128]{1,0:T(8,128)S(1)} %get-tuple-element.7.surge_in) | copy-start | bytes 98308

commit v6 on v5

--- a/solution.py
+++ b/solution.py
@@ -13,6 +13,7 @@
 KAPPA = 0.08
 LANES = 128
 HALO = 8
+PARTS = 2
 
 
 def kernel(
@@ -100,8 +101,12 @@
 
     pl.semaphore_wait(barrier, 5 + groups - 1)
 
+    pieces = tiles_dev * PARTS
+    piece_rows = grid_ref.shape[1] // PARTS
+
     def tile_of(where, which_core, t):
-        return grid_ref.at[device_at(where, which_core) * tiles_dev + t]
+        tile = device_at(where, which_core) * tiles_dev + t // PARTS
+        return grid_ref.at[tile, pl.ds(t % PARTS * piece_rows, piece_rows)]
 
     def ring_copy(way, far, t):
         where = place - far + 1 if way == 0 else place + far - 1
@@ -131,7 +136,7 @@
         )
 
     def reach(way, t):
-        return half if t % 2 == way else half - 1
+        return half if t // (pieces // 2) == way else half - 1
 
     sent = []
 
@@ -139,15 +144,13 @@
         copy.start()
         sent.append(copy)
 
-    waves = [[(way, (way + s) % tiles_dev) for way in range(2)] for s in range(tiles_dev)]
-
-    def begin(wave):
-        copies = [ring_copy(way, 1, t) for way, t in wave if reach(way, t) >= 1]
-        for copy in copies:
-            copy.start()
-        return copies
-
-    started = begin(waves[0])
+    waves = [[(way, (way * (pieces // 2) + s) % pieces) for way in range(2)] for s in range(pieces)]
+    for wave in waves:
+        for way, t in wave:
+            if reach(way, t) >= 1:
+                start(ring_copy(way, 1, t))
+    for t in range(pieces):
+        start(sibling_copy(0, 0, t, core))
 
     ends = ((after, length - HALO, 0, 0), (before, 0, HALO + length, 1))
     halo = []
@@ -225,16 +228,8 @@
         def _(i):
             weights(j, i)
 
-    for n, wave in enumerate(waves):
-        for copy in started:
-            copy.wait_send()
-        if n + 1 < tiles_dev:
-            started = begin(waves[n + 1])
-        if n == 0:
-            for t in range(tiles_dev):
-                start(sibling_copy(0, 0, t, core))
-            node_rows(0, data_ref.at[0])
-            group_weights(0)
+    node_rows(0, data_ref.at[0])
+    group_weights(0)
 
     def await_asked(j):
         node, need = asked[j - 1]
@@ -293,11 +288,11 @@
                 start(ring_copy(way, far + 1, t))
         for way, far, t in batch:
             start(sibling_copy(way, far, t, core))
-        until = min(n, len(work)) if n + 1 < len(events) else len(work)
+        until = min(n // PARTS, len(work)) if n + 1 < len(events) else len(work)
         for item in work[done:until]:
             item()
         done = until
-    for t in range(tiles_dev):
+    for t in range(pieces):
         sibling_copy(0, 0, t, 1 - core).wait_recv()
     for way, far, t in sum(events, []):
         sibling_copy(way, far, t, 1 - core).wait_recv()
@@ -382,17 +377,6 @@
             answer(j, m).wait_send()
 
 
-def hand_over(forcing_in, surge_in, forcing_out, surge_out, sem):
-    copies = [
-        pltpu.make_async_copy(forcing_in, forcing_out, sem.at[0]),
-        pltpu.make_async_copy(surge_in, surge_out, sem.at[1]),
-    ]
-    for copy in copies:
-        copy.start()
-    for copy in copies:
-        copy.wait()
-
-
 def shards(
     background, storm_track, need_tiles, node_cells, node_fracs, slot_count, elevation, bed_level
 ):
@@ -406,6 +390,7 @@
     pairs = cell_count // LANES
     length = elevation.shape[1] // LANES
     others = max(groups - 1, 1)
+    pieces = tiles_dev * PARTS
     vmem = pl.BlockSpec(memory_space=pltpu.VMEM)
     hbm = pl.BlockSpec(memory_space=pltpu.HBM)
     dma = pltpu.SemaphoreType.DMA
@@ -440,8 +425,8 @@
             pltpu.VMEM((fields, slots, positions), jnp.float32),
             pltpu.VMEM((others, per_band // 2, 16, positions), jnp.bfloat16),
             pltpu.VMEM((others, per_band // 2, 16, positions), jnp.bfloat16),
-            dma((2, half, tiles_dev)), dma((2, half, tiles_dev)),
-            dma((2, half + 1, tiles_dev)), dma((2, half + 1, tiles_dev)),
+            dma((2, half, pieces)), dma((2, half, pieces)),
+            dma((2, half + 1, pieces)), dma((2, half + 1, pieces)),
             dma((2, 2)), dma((2, 2)),
             dma((groups,)), dma((groups,)),
             dma((groups,)), dma((groups,)), dma((groups,)),
@@ -458,16 +443,6 @@
         node_cells, node_fracs,
         elevation.reshape(length, LANES), bed_level.reshape(length, LANES),
     )
-    forcing, surge = pl.pallas_call(
-        hand_over,
-        out_shape=(
-            jax.ShapeDtypeStruct(forcing.shape, forcing.dtype),
-            jax.ShapeDtypeStruct(surge.shape, surge.dtype),
-        ),
-        in_specs=[vmem] * 2,
-        out_specs=(hbm, hbm),
-        scratch_shapes=[dma((2,))],
-    )(forcing, surge)
     return forcing.transpose(1, 0, 2), surge.reshape(1, -1)
 
 

time: 27.9 us -> 26.6 us (0.953)
  Pallas kernels: 25.9 us -> 24.5 us
    pallas_call x1 -> x0, Pallas kernels: 1.56 us -> none  [shards(): pl.pallas_call(hand_over, out_shape=(jax.ShapeDtypeStruct(forcing.shape,...]
    unnamed x4 -> x2, local copies, waits for them, and re-layouts: 1.23 us -> 1.26 us
where the time goes in v6:
time: 26.6 us; the launch traced here: 26.4 us
  Pallas kernels  24.5 us (92%)
  local copies, waits for them, and re-layouts  1.26 us (5%)
  between operations  0.64 us (2%)
    pallas_call x1, Pallas kernels, shards(): pl.pallas_call(functools.partial(kernel, groups, holders), out_shape=(plt...  24.5 us
    unnamed x2, local copies, waits for them, and re-layouts  1.26 us

profile of v6, /device:TPU:0, one launch (start us, length us, event | category | flops | bytes accessed | tf_op | source)
XLA Modules:
  0.0 26.4 jit_solution(12267867930311304237)
XLA Ops:
  0.6 24.5 %shard_map.95 = (bf16[6,8,1024]{2,1,0:T(8,128)(2,1)S(1)}, f32[64,128]{1,0:T(8,128)S(1)}) custom-call(f32[2,5]{1,0:T(2,128)} %storm_hbm.1, s32[1,8]{1,0:T(1,128)} %need_hbm.1, s32[1,8]{1,0:T(1,128)} %bitcast.15, bf16[384,128]{1,0:T(8,128)(2,1)} %bitcast.12, s32[8,1024]{1,0:T(8,128)} %cells_hbm.1, f32[2,8,1024]{2,1,0:T(8,128)} %fracs_hbm.1, ...), custom_call_target="tpu_custom_call" | custom-call | tf_op jit(solution)/shard_map/pallas_call | solution.py:397
  25.2 0.6 %copy.13 = bf16[8,6,1024]{2,0,1:T(8,128)(2,1)} copy(bf16[8,6,1024]{2,0,1:T(8,128)(2,1)S(1)} %bitcast.10) | data formatting | bytes 196608
  25.8 0.6 %copy.14 = f32[1,8192]{1,0:T(1,128)} copy(f32[1,8192]{1,0:T(1,128)S(1)} %bitcast.11) | data formatting | bytes 65536

commit v7 on v6

--- a/solution.py
+++ b/solution.py
@@ -223,13 +223,13 @@
                 row == row_first, upper, jnp.where(row == row_first + 1, lower, 0.0)
             )
 
-    def group_weights(j):
-        @pl.loop(0, per_band)
+    def some_weights(j, part):
+        @pl.loop(part * (per_band // 2), (part + 1) * (per_band // 2))
         def _(i):
             weights(j, i)
 
     node_rows(0, data_ref.at[0])
-    group_weights(0)
+    some_weights(0, 0)
 
     def await_asked(j):
         node, need = asked[j - 1]
@@ -269,32 +269,37 @@
             surface = surface - (flux - shifted(flux, 1))
         surf_ref[...] = surface
 
-    work = [sweep]
-    for j in range(1, groups):
-        work.append(functools.partial(await_asked, j))
-        work.append(functools.partial(group_weights, j))
+    work = [functools.partial(some_weights, 0, 1)]
+    for j in range(1, groups):
+        work.append(lambda j=j: (await_asked(j), some_weights(j, 0)))
+        work.append(functools.partial(some_weights, j, 1))
 
     events = [
-        [(way, far, t) for way, t in wave if far <= reach(way, t)]
+        [[(way, far, t) for way, t in wave if far <= reach(way, t)] for wave in waves]
         for far in range(1, half + 1)
-        for wave in waves
     ]
-    events = [batch for batch in events if batch]
     done = 0
-    for n, batch in enumerate(events):
-        for way, far, t in batch:
-            ring_arrival(way, far, t).wait_recv()
-            if far < reach(way, t):
-                start(ring_copy(way, far + 1, t))
-        for way, far, t in batch:
-            start(sibling_copy(way, far, t, core))
-        until = min(n // PARTS, len(work)) if n + 1 < len(events) else len(work)
-        for item in work[done:until]:
+    for n, hop in enumerate(events):
+        for batch in hop:
+            for way, far, t in batch:
+                ring_arrival(way, far, t).wait_recv()
+                if far < reach(way, t):
+                    start(ring_copy(way, far + 1, t))
+            for way, far, t in batch:
+                start(sibling_copy(way, far, t, core))
+        if n + 1 < half:
+            until = (n + 1) * len(work) // (half - 1)
+            for item in work[done:until]:
+                item()
+            done = until
+            if n + 2 == half:
+                sweep()
+    if half == 1:
+        for item in work + [sweep]:
             item()
-        done = until
     for t in range(pieces):
         sibling_copy(0, 0, t, 1 - core).wait_recv()
-    for way, far, t in sum(events, []):
+    for way, far, t in sum(sum(events, []), []):
         sibling_copy(way, far, t, 1 - core).wait_recv()
 
     chunk = 256

time: 26.6 us -> 26.2 us (0.985)
  Pallas kernels: 24.5 us -> 24.1 us
    pallas_call x1, Pallas kernels: 24.5 us -> 24.1 us  [shards(): pl.pallas_call(functools.partial(kernel, groups, holders), out_shape=(plt...]
where the time goes in v7:
time: 26.2 us; the launch traced here: 26 us
  Pallas kernels  24.1 us (92%)
  local copies, waits for them, and re-layouts  1.26 us (5%)
  between operations  0.64 us (2%)
    pallas_call x1, Pallas kernels, shards(): pl.pallas_call(functools.partial(kernel, groups, holders), out_shape=(plt...  24.1 us
    unnamed x2, local copies, waits for them, and re-layouts  1.26 us

profile of v7, /device:TPU:0, one launch (start us, length us, event | category | flops | bytes accessed | tf_op | source)
XLA Modules:
  0.0 26.0 jit_solution(17001730505621033409)
XLA Ops:
  0.6 24.1 %shard_map.95 = (bf16[6,8,1024]{2,1,0:T(8,128)(2,1)S(1)}, f32[64,128]{1,0:T(8,128)S(1)}) custom-call(f32[2,5]{1,0:T(2,128)} %storm_hbm.1, s32[1,8]{1,0:T(1,128)} %need_hbm.1, s32[1,8]{1,0:T(1,128)} %bitcast.15, bf16[384,128]{1,0:T(8,128)(2,1)} %bitcast.12, s32[8,1024]{1,0:T(8,128)} %cells_hbm.1, f32[2,8,1024]{2,1,0:T(8,128)} %fracs_hbm.1, ...), custom_call_target="tpu_custom_call" | custom-call | tf_op jit(solution)/shard_map/pallas_call | solution.py:402
  24.8 0.6 %copy.13 = bf16[8,6,1024]{2,0,1:T(8,128)(2,1)} copy(bf16[8,6,1024]{2,0,1:T(8,128)(2,1)S(1)} %bitcast.10) | data formatting | bytes 196608
  25.4 0.6 %copy.14 = f32[1,8192]{1,0:T(1,128)} copy(f32[1,8192]{1,0:T(1,128)S(1)} %bitcast.11) | data formatting | bytes 65536
